TPU v7x, 32 devices: a whole 2x2x4 slice. The times are simulated.
32 devices in a mesh: ctx: 16 (over z, y, x), head: 2 (over core).
Axes of the slice: x: 2, y: 2, z: 4, core: 2. Of those that a mesh axis runs over, the one named last changes fastest.
Arguments:
- lin_q: bfloat16 [8192, 8, 128], P('ctx', 'head'), may hold values from -1.5 to 1.5
- lin_k: bfloat16 [8192, 8, 128], P('ctx', 'head'), may hold values from -1.5 to 1.5
- lin_v: bfloat16 [8192, 8, 128], P('ctx', 'head'), may hold values from -3 to 3
- lin_dout: bfloat16 [8192, 8, 128], P('ctx', 'head'), may hold values from -0.29882812 to 0.29882812
- lin_decay: float32 [8, 8192], P('head', 'ctx'), may hold values from -1 to 0
- att_q: bfloat16 [8192, 8, 128], P('ctx', 'head'), may hold values from -64 to 64
- att_k: bfloat16 [8192, 128], P('ctx'), may hold values from -6 to 6
- att_v: bfloat16 [8192, 128], P('ctx'), may hold values from -6 to 6
- att_dout: bfloat16 [8192, 8, 128], P('ctx', 'head'), may hold values from -1.796875 to 1.796875
- doc_block: int32 [32], replicated, may hold values from 0 to 4, as said below
Outputs:
- lin_dq: bfloat16 [8192, 8, 128], P('ctx', 'head')
- lin_dk: bfloat16 [8192, 8, 128], P('ctx', 'head')
- lin_dv: bfloat16 [8192, 8, 128], P('ctx', 'head')
- att_dq: bfloat16 [8192, 8, 128], P('ctx', 'head')
- att_dk: bfloat16 [8192, 128], P(('ctx', 'head'))
- att_dv: bfloat16 [8192, 128], P(('ctx', 'head'))
Inputs may be any that keep to these rules, and one draw needn't show every extreme that they name: doc_block starts at 0, never falls and rises by at most one from block to block; each document spans 1 to 12 blocks; the first spans exactly 12.
All inputs are finite; a program needn't handle non-finite values.
Results may differ from a plain program's by a relative error of at most 0.0052.
Values may be sent and summed in bfloat16 or wider, within the bound.
A program may use at most 128 MiB of HBM per device.

v0:
```python
import jax
import jax.numpy as jnp
from jax import lax
from jax.sharding import PartitionSpec as P

TILE_WIDTH = 256
REACH = 6


NEG = -1e30


def shifted(value, axis, steps):
    count = lax.axis_size(axis)
    first, last = (max(0, -steps), min(count, count - steps))
    return lax.ppermute(value, axis, [(source, source + steps) for source in range(first, last)])


def as_sent(x):
    return jax.tree.map(lambda a: a.astype(jnp.bfloat16) if a.dtype == jnp.float32 else a, x)


def shifted_2(value, axis, steps):
    count = lax.axis_size(axis)
    pairs = [(source, (source + steps) % count) for source in range(count)]
    return lax.ppermute(value, axis, pairs)


def block_terms(queries, keys_in, values, douts, decay):
    highest = lax.Precision.HIGHEST
    cumulative = jnp.cumsum(decay, axis=1)
    block_total = cumulative[:, -1]
    offsets = jnp.arange(decay.shape[1], dtype=jnp.int32)
    lower_tri = (offsets[:, None] >= offsets[None, :])[None]
    spread = jnp.where(lower_tri, cumulative[:, :, None] - cumulative[:, None, :], 0.0)
    weights = jnp.where(lower_tri, jnp.exp(spread), 0.0)
    cross = jnp.einsum("thd,shd->hts", douts, values, preferred_element_type=jnp.float32)
    inner = jnp.einsum("thd,shd->hts", queries, keys_in, preferred_element_type=jnp.float32)
    left_mix = (cross * weights).astype(jnp.bfloat16)
    right_mix = (inner * weights).astype(jnp.bfloat16)
    grad_query = jnp.einsum("hts,shd->thd", left_mix, keys_in, preferred_element_type=jnp.float32)
    grad_key = jnp.einsum("hts,thd->shd", left_mix, queries, preferred_element_type=jnp.float32)
    grad_value = jnp.einsum("hts,thd->shd", right_mix, douts, preferred_element_type=jnp.float32)
    head_decay = jnp.exp(cumulative).T[:, :, None]
    tail_decay = jnp.exp(block_total[:, None] - cumulative).T[:, :, None]
    key_state = jnp.einsum(
        "shi,shj->hij",
        keys_in.astype(jnp.float32) * tail_decay,
        values.astype(jnp.float32),
        precision=highest,
    )
    query_state = jnp.einsum(
        "thi,thj->hij",
        queries.astype(jnp.float32) * head_decay,
        douts.astype(jnp.float32),
        precision=highest,
    )
    return (
        grad_query,
        grad_key,
        grad_value,
        head_decay,
        tail_decay,
        block_total,
        key_state,
        query_state,
    )


def finish(terms, keys_in, values, douts, into, back):
    highest = lax.Precision.HIGHEST
    (
        grad_query,
        grad_key,
        grad_value,
        head_decay,
        tail_decay,
        block_total,
        key_state,
        query_state,
    ) = terms
    grad_query = grad_query + head_decay * jnp.einsum(
        "thj,hij->thi", douts.astype(jnp.float32), into, precision=highest
    )
    grad_key = grad_key + tail_decay * jnp.einsum(
        "shj,hij->shi", values.astype(jnp.float32), back, precision=highest
    )
    grad_value = grad_value + tail_decay * jnp.einsum(
        "shi,hij->shj", keys_in.astype(jnp.float32), back, precision=highest
    )
    return (
        grad_query.astype(jnp.bfloat16),
        grad_key.astype(jnp.bfloat16),
        grad_value.astype(jnp.bfloat16),
    )


def lightning(lin_q, lin_k, lin_v, lin_dout, lin_decay, doc_block, device_index):
    length, heads, width = lin_q.shape
    nblocks = length // TILE_WIDTH
    block_shape = (nblocks, TILE_WIDTH, heads, width)
    queries = lin_q.reshape(block_shape)
    keys_in = lin_k.reshape(block_shape)
    values = lin_v.reshape(block_shape)
    douts = lin_dout.reshape(block_shape)
    decay = lin_decay.reshape(heads, nblocks, TILE_WIDTH).transpose(1, 0, 2)
    terms = jax.vmap(block_terms)(queries, keys_in, values, douts, decay)
    block_total, key_state, query_state = (terms[5], terms[6], terms[7])
    padded_doc = jnp.concatenate(
        [jnp.full((1,), -1, jnp.int32), doc_block, jnp.full((1,), -2, jnp.int32)]
    )
    near_doc = lax.dynamic_slice_in_dim(padded_doc, device_index * nblocks, nblocks + 2)
    follows = (near_doc[1:-1] == near_doc[:-2]).astype(jnp.float32)
    precedes = (near_doc[2:] == near_doc[1:-1]).astype(jnp.float32)
    keep = jnp.exp(block_total)

    def forward_pass(state_in):
        entries = []
        for index in range(nblocks):
            entering = follows[index] * state_in
            entries.append(entering)
            state_in = key_state[index] + keep[index][:, None, None] * entering
        return (jnp.stack(entries), state_in)

    def backward_pass(state_in):
        entries = [None] * nblocks
        for index in reversed(range(nblocks)):
            entering = precedes[index] * state_in
            entries[index] = entering
            state_in = query_state[index] + keep[index][:, None, None] * entering
        return (jnp.stack(entries), state_in)

    zero_state = jnp.zeros((heads, width, width), jnp.float32)
    unused_one, left_total = forward_pass(zero_state)
    unused_two, right_total = backward_pass(zero_state)
    left_mult = jnp.prod(keep * follows[:, None], axis=0)
    right_mult = jnp.prod(keep * precedes[:, None], axis=0)

    def relay(section, carried):
        from_left, from_right = carried
        from_left = shifted(left_mult[:, None, None] * from_left + left_total, "ctx", 1)
        from_right = shifted(right_mult[:, None, None] * from_right + right_total, "ctx", -1)
        return (from_left, from_right)

    from_left, from_right = lax.fori_loop(0, REACH, relay, (zero_state, zero_state))
    into_all, unused_three = forward_pass(from_left)
    back_all, unused_four = backward_pass(from_right)
    grads = jax.vmap(finish)(terms, keys_in, values, douts, into_all, back_all)
    return tuple((grad.reshape(length, heads, width) for grad in grads))


def attention(att_q, att_k, att_v, att_dout, doc_block, device_index, devices):
    length, qheads, width = att_q.shape
    nblocks = length // TILE_WIDTH
    scale = width ** (-0.5)
    offsets = jnp.arange(length, dtype=jnp.int32)

    def docs_of(device):
        return jnp.repeat(
            lax.dynamic_slice_in_dim(doc_block, device * nblocks, nblocks), TILE_WIDTH
        )

    query_doc = docs_of(device_index)
    query_pos = device_index * length + offsets

    def visible_pairs(device):
        key_doc = docs_of(device)
        key_pos = device * length + offsets
        return (query_doc[:, None] == key_doc[None, :]) & (key_pos[None, :] <= query_pos[:, None])

    def gather_stats(stats, key_pair, device):
        keys_in, values = key_pair
        visible = visible_pairs(device)
        running_max, running_sum, weighted = stats
        scores = (
            jnp.einsum("thd,sd->hts", att_q, keys_in, preferred_element_type=jnp.float32) * scale
        )
        scores = jnp.where(visible[None], scores, NEG)
        grad_probs = jnp.einsum("thd,sd->hts", att_dout, values, preferred_element_type=jnp.float32)
        new_max = jnp.maximum(running_max, jnp.max(scores, axis=2))
        plain = jnp.where(visible[None], jnp.exp(scores - new_max[:, :, None]), 0.0)
        factor = jnp.exp(running_max - new_max)
        return (
            new_max,
            running_sum * factor + jnp.sum(plain, axis=2),
            weighted * factor + jnp.sum(plain * grad_probs, axis=2),
        )

    key_pair = (att_k, att_v)
    zero_rows = jnp.zeros((qheads, length), jnp.float32)
    stats = gather_stats(
        (jnp.full((qheads, length), NEG, jnp.float32), zero_rows, zero_rows), key_pair, device_index
    )

    def stat_section(section, carried):
        stats_in, pair_in = carried
        pair_in = jax.tree.map(
            lambda part, own: part.astype(own.dtype), shifted(as_sent(pair_in), "ctx", 1), pair_in
        )
        device = (device_index - section) % devices
        return (gather_stats(stats_in, pair_in, device), pair_in)

    stats, unused_pair = lax.fori_loop(1, REACH + 1, stat_section, (stats, key_pair))
    running_max, running_sum, weighted = stats
    lse = running_max + jnp.log(running_sum)
    delta = weighted / running_sum

    def grad_terms(pair_in, device):
        keys_in, values = pair_in
        visible = visible_pairs(device)
        scores = (
            jnp.einsum("thd,sd->hts", att_q, keys_in, preferred_element_type=jnp.float32) * scale
        )
        probs = jnp.where(visible[None], jnp.exp(scores - lse[:, :, None]), 0.0)
        grad_probs = jnp.einsum("thd,sd->hts", att_dout, values, preferred_element_type=jnp.float32)
        grad_scores = probs * (grad_probs - delta[:, :, None])
        probs_b = probs.astype(jnp.bfloat16)
        grad_b = grad_scores.astype(jnp.bfloat16)
        part_query = jnp.einsum("hts,sd->thd", grad_b, keys_in, preferred_element_type=jnp.float32)
        part_key = jnp.einsum("hts,thd->sd", grad_b, att_q, preferred_element_type=jnp.float32)
        part_value = jnp.einsum(
            "hts,thd->sd", probs_b, att_dout, preferred_element_type=jnp.float32
        )
        return (part_query, jnp.stack([part_key, part_value]))

    part_query, part_pair = grad_terms(key_pair, device_index)
    travel = part_pair

    def grad_section(section, carried):
        grad_query, pair_in, travel_in = carried
        pair_in = jax.tree.map(
            lambda part, own: part.astype(own.dtype), shifted(as_sent(pair_in), "ctx", 1), pair_in
        )
        travel_in = shifted_2(travel_in, "ctx", 1)
        device = (device_index - section) % devices
        more_query, more_pair = grad_terms(pair_in, device)
        return (grad_query + more_query, pair_in, travel_in + more_pair)

    grad_query, unused_keys, travel = lax.fori_loop(
        1, REACH + 1, grad_section, (part_query, key_pair, travel)
    )
    travel = shifted_2(travel, "ctx", -REACH)
    travel = lax.psum_scatter(travel, "head", scatter_dimension=1, tiled=True)
    att_dq = (grad_query * scale).astype(jnp.bfloat16)
    att_dk = (travel[0] * scale).astype(jnp.bfloat16)
    att_dv = travel[1].astype(jnp.bfloat16)
    return (att_dq, att_dk, att_dv)


def shards(lin_q, lin_k, lin_v, lin_dout, lin_decay, att_q, att_k, att_v, att_dout, doc_block):
    device_index = lax.axis_index("ctx")
    devices = lax.axis_size("ctx")
    lin_dq, lin_dk, lin_dv = lightning(
        lin_q, lin_k, lin_v, lin_dout, lin_decay, doc_block, device_index
    )
    att_dq, att_dk, att_dv = attention(
        att_q, att_k, att_v, att_dout, doc_block, device_index, devices
    )
    return (lin_dq, lin_dk, lin_dv, att_dq, att_dk, att_dv)


def solution(mesh):
    return jax.shard_map(
        shards,
        mesh=mesh,
        in_specs=(
            P("ctx", "head", None),
            P("ctx", "head", None),
            P("ctx", "head", None),
            P("ctx", "head", None),
            P("head", "ctx"),
            P("ctx", "head", None),
            P("ctx", None),
            P("ctx", None),
            P("ctx", "head", None),
            P(),
        ),
        out_specs=(
            P("ctx", "head", None),
            P("ctx", "head", None),
            P("ctx", "head", None),
            P("ctx", "head", None),
            P(("ctx", "head"), None),
            P(("ctx", "head"), None),
        ),
        check_vma=False,
    )
```

profile of v0, /device:TPU:7, one launch (start us, length us, event | category | flops | bytes accessed | tf_op | source)
XLA Modules:
  0.0 368.3 jit_solution(6854011443588273121)
XLA Ops:
  12.0 1.9 fusion.41
  15.1 4.7 %fusion.36 = (f32[4,512]{1,0:T(4,128)S(1)}, f32[4,512]{1,0:T(4,128)S(1)}, f32[512,512,4]{1,0,2:T(8,128)}) fusion(f32[512,512,4]{1,0,2:T(8,128)S(1)} %get-tuple-element.908, f32[4,512]{1,0:T(4,128)S(1)} %broadcast_maximum_fusion, pred[512,512]{0,1:T(8,128)(4,1)S(1)} %compare_and_fusion.2, bf16[512,4,128]{2,1,0:T(4,128)(2,1)S(1)} %copy-done.12, ...), kind=kOutput, calls=%fused_computation.52 | convolution fusion | flops 275771392 | bytes 9330688 | tf_op jit(solution)/shard_map/thd,sd->hts/dot_general | solution.py:179
  19.9 71.1 %while.59 = (s32[]{:T(128)}, f32[4,512]{1,0:T(4,128)S(1)}, f32[4,512]{1,0:T(4,128)S(1)}, f32[4,512]{1,0:T(4,128)S(1)}, bf16[512,128]{1,0:T(8,128)(2,1)S(1)}, /*i...) while((s32[]{:T(128)}, f32[4,512]{1,0:T(4,128)S(1)}, ...), condition=%wide.region_13.14_spmd.clone, body=%wide.region_9.13_spmd.clone.sunk | while | flops 552344576 | bytes 16687580 | solution.py:203
  19.9 3.1 collective-permute-start.2
  23.0 3.1 collective-permute-start.3
  30.4 4.9 %collective-permute-start.2 = (bf16[512,128]{1,0:T(8,128)(2,1)S(1)}, bf16[512,128]{1,0:T(8,128)(2,1)S(1)}, u32[]{:S(2)}, u32[]{:S(2)}) collective-permute-start(bf16[512,128]{1,0:T(8,128)(2,1)S(1)} %get-tuple-element.1166), channel_id=1, source_target_pairs={{0,2},{2,4},{4,6},{6,8},{8,10},{10,12},{12,14},{14,16},{16,18},{18... | collective-permute-start | bytes 393224 | tf_op jit(solution)/shard_map/while/body/eval_jaxpr/ppermute | solution.py:16
  35.4 1.9 collective-permute-start.3
  42.8 4.8 %collective-permute-start.2 = (bf16[512,128]{1,0:T(8,128)(2,1)S(1)}, bf16[512,128]{1,0:T(8,128)(2,1)S(1)}, u32[]{:S(2)}, u32[]{:S(2)}) collective-permute-start(bf16[512,128]{1,0:T(8,128)(2,1)S(1)} %get-tuple-element.1166), channel_id=1, source_target_pairs={{0,2},{2,4},{4,6},{6,8},{8,10},{10,12},{12,14},{14,16},{16,18},{18... | collective-permute-start | bytes 393224 | tf_op jit(solution)/shard_map/while/body/eval_jaxpr/ppermute | solution.py:16
  47.6 1.9 collective-permute-start.3
  55.6 3.2 collective-permute-start.2
  58.8 2.9 collective-permute-start.3
  66.8 4.1 %collective-permute-start.2 = (bf16[512,128]{1,0:T(8,128)(2,1)S(1)}, bf16[512,128]{1,0:T(8,128)(2,1)S(1)}, u32[]{:S(2)}, u32[]{:S(2)}) collective-permute-start(bf16[512,128]{1,0:T(8,128)(2,1)S(1)} %get-tuple-element.1166), channel_id=1, source_target_pairs={{0,2},{2,4},{4,6},{6,8},{8,10},{10,12},{12,14},{14,16},{16,18},{18... | collective-permute-start | bytes 393224 | tf_op jit(solution)/shard_map/while/body/eval_jaxpr/ppermute | solution.py:16
  70.9 3.1 collective-permute-start.3
  78.7 4.5 %collective-permute-start.2 = (bf16[512,128]{1,0:T(8,128)(2,1)S(1)}, bf16[512,128]{1,0:T(8,128)(2,1)S(1)}, u32[]{:S(2)}, u32[]{:S(2)}) collective-permute-start(bf16[512,128]{1,0:T(8,128)(2,1)S(1)} %get-tuple-element.1166), channel_id=1, source_target_pairs={{0,2},{2,4},{4,6},{6,8},{8,10},{10,12},{12,14},{14,16},{16,18},{18... | collective-permute-start | bytes 393224 | tf_op jit(solution)/shard_map/while/body/eval_jaxpr/ppermute | solution.py:16
  83.2 2.5 collective-permute-start.3
  91.0 3.3 fusion.58
  94.6 3.5 fusion.38
  100.5 127.6 %while.60 = (s32[]{:T(128)}, f32[512,4,128]{2,0,1:T(8,128)S(1)}, bf16[512,128]{1,0:T(8,128)(2,1)S(1)}, bf16[512,128]{1,0:T(8,128)(2,1)}, f32[2,512,128]{2,1,0:T(...) while((s32[]{:T(128)}, f32[512,4,128]{2,0,1:T(8,128)S(1)}, ...), condition=%wide.region_15.16_spmd.clone, body=%wide.region_14.15_spmd.clone.sunk | while | flops 1353974784 | bytes 32195140 | solution.py:239
  100.5 4.0 %collective-permute-start.4 = (bf16[512,128]{1,0:T(8,128)(2,1)S(1)}, bf16[512,128]{1,0:T(8,128)(2,1)S(1)}, u32[]{:S(2)}, u32[]{:S(2)}) collective-permute-start(bf16[512,128]{1,0:T(8,128)(2,1)S(1)} %get-tuple-element.1222), channel_id=1, source_target_pairs={{0,2},{2,4},{4,6},{6,8},{8,10},{10,12},{12,14},{14,16},{16,18},{18... | collective-permute-start | bytes 393224 | tf_op jit(solution)/shard_map/while/body/eval_jaxpr/ppermute | solution.py:16
  104.5 1.9 collective-permute-start.5
  115.2 3.9 %collective-permute-done.6 = f32[2,512,128]{2,1,0:T(8,128)S(1)} collective-permute-done((f32[2,512,128]{2,1,0:T(8,128)}, f32[2,512,128]{2,1,0:T(8,128)S(1)}, u32[]{:S(2)}, u32[]{:S(2)}) %collective-permute-start.6) | collective-permute-done | bytes 524320 | tf_op jit(solution)/shard_map/while/body/eval_jaxpr/ppermute | solution.py:26
  120.0 3.3 collective-permute-start.4
  123.3 3.0 collective-permute-start.5
  126.3 3.0 collective-permute-start.6
  136.0 4.8 %collective-permute-done.6 = f32[2,512,128]{2,1,0:T(8,128)S(1)} collective-permute-done((f32[2,512,128]{2,1,0:T(8,128)}, f32[2,512,128]{2,1,0:T(8,128)S(1)}, u32[]{:S(2)}, u32[]{:S(2)}) %collective-permute-start.6) | collective-permute-done | bytes 524320 | tf_op jit(solution)/shard_map/while/body/eval_jaxpr/ppermute | solution.py:26
  141.7 5.8 %collective-permute-start.4 = (bf16[512,128]{1,0:T(8,128)(2,1)S(1)}, bf16[512,128]{1,0:T(8,128)(2,1)S(1)}, u32[]{:S(2)}, u32[]{:S(2)}) collective-permute-start(bf16[512,128]{1,0:T(8,128)(2,1)S(1)} %get-tuple-element.1222), channel_id=1, source_target_pairs={{0,2},{2,4},{4,6},{6,8},{8,10},{10,12},{12,14},{14,16},{16,18},{18... | collective-permute-start | bytes 393224 | tf_op jit(solution)/shard_map/while/body/eval_jaxpr/ppermute | solution.py:16
  151.4 2.0 collective-permute-done.5
  158.2 3.9 %collective-permute-done.6 = f32[2,512,128]{2,1,0:T(8,128)S(1)} collective-permute-done((f32[2,512,128]{2,1,0:T(8,128)}, f32[2,512,128]{2,1,0:T(8,128)S(1)}, u32[]{:S(2)}, u32[]{:S(2)}) %collective-permute-start.6) | collective-permute-done | bytes 524320 | tf_op jit(solution)/shard_map/while/body/eval_jaxpr/ppermute | solution.py:26
  162.9 5.8 %collective-permute-start.4 = (bf16[512,128]{1,0:T(8,128)(2,1)S(1)}, bf16[512,128]{1,0:T(8,128)(2,1)S(1)}, u32[]{:S(2)}, u32[]{:S(2)}) collective-permute-start(bf16[512,128]{1,0:T(8,128)(2,1)S(1)} %get-tuple-element.1222), channel_id=1, source_target_pairs={{0,2},{2,4},{4,6},{6,8},{8,10},{10,12},{12,14},{14,16},{16,18},{18... | collective-permute-start | bytes 393224 | tf_op jit(solution)/shard_map/while/body/eval_jaxpr/ppermute | solution.py:16
  172.7 2.5 collective-permute-done.5
  179.9 3.9 %collective-permute-done.6 = f32[2,512,128]{2,1,0:T(8,128)S(1)} collective-permute-done((f32[2,512,128]{2,1,0:T(8,128)}, f32[2,512,128]{2,1,0:T(8,128)S(1)}, u32[]{:S(2)}, u32[]{:S(2)}) %collective-permute-start.6) | collective-permute-done | bytes 524320 | tf_op jit(solution)/shard_map/while/body/eval_jaxpr/ppermute | solution.py:26
  184.7 5.1 %collective-permute-start.4 = (bf16[512,128]{1,0:T(8,128)(2,1)S(1)}, bf16[512,128]{1,0:T(8,128)(2,1)S(1)}, u32[]{:S(2)}, u32[]{:S(2)}) collective-permute-start(bf16[512,128]{1,0:T(8,128)(2,1)S(1)} %get-tuple-element.1222), channel_id=1, source_target_pairs={{0,2},{2,4},{4,6},{6,8},{8,10},{10,12},{12,14},{14,16},{16,18},{18... | collective-permute-start | bytes 393224 | tf_op jit(solution)/shard_map/while/body/eval_jaxpr/ppermute | solution.py:16
  194.1 2.9 collective-permute-done.5
  201.8 4.3 %collective-permute-done.6 = f32[2,512,128]{2,1,0:T(8,128)S(1)} collective-permute-done((f32[2,512,128]{2,1,0:T(8,128)}, f32[2,512,128]{2,1,0:T(8,128)S(1)}, u32[]{:S(2)}, u32[]{:S(2)}) %collective-permute-start.6) | collective-permute-done | bytes 524320 | tf_op jit(solution)/shard_map/while/body/eval_jaxpr/ppermute | solution.py:26
  207.0 3.7 %collective-permute-start.4 = (bf16[512,128]{1,0:T(8,128)(2,1)S(1)}, bf16[512,128]{1,0:T(8,128)(2,1)S(1)}, u32[]{:S(2)}, u32[]{:S(2)}) collective-permute-start(bf16[512,128]{1,0:T(8,128)(2,1)S(1)} %get-tuple-element.1222), channel_id=1, source_target_pairs={{0,2},{2,4},{4,6},{6,8},{8,10},{10,12},{12,14},{14,16},{16,18},{18... | collective-permute-start | bytes 393224 | tf_op jit(solution)/shard_map/while/body/eval_jaxpr/ppermute | solution.py:16
  215.4 2.3 collective-permute-done.5
  222.4 4.8 %collective-permute-done.6 = f32[2,512,128]{2,1,0:T(8,128)S(1)} collective-permute-done((f32[2,512,128]{2,1,0:T(8,128)}, f32[2,512,128]{2,1,0:T(8,128)S(1)}, u32[]{:S(2)}, u32[]{:S(2)}) %collective-permute-start.6) | collective-permute-done | bytes 524320 | tf_op jit(solution)/shard_map/while/body/eval_jaxpr/ppermute | solution.py:26
  229.7 2.4 reduce-window.6
  236.1 2.6 fusion.62
  238.7 3.3 fusion.48
  242.0 2.7 multiply_convert_fusion.1
  248.9 86.4 %while.58 = (s32[]{:T(128)}, f32[4,128,128]{2,1,0:T(8,128)S(1)}, f32[4,128,128]{2,1,0:T(8,128)S(1)}, f32[4]{0:T(128)S(1)}, f32[4,128,128]{2,1,0:T(8,128)S(1)}, /...) while((s32[]{:T(128)}, f32[4,128,128]{2,1,0:T(8,128)S(1)}, f32[4,128,128]{2,1,0:T(8,128)S(1)}, ...), condition=%wide.region_5.6_spmd, body=%wide.region_4.5_spmd.sunk | while | flops 262146 | bytes 3670213 | solution.py:145
  249.0 3.3 collective-permute-start
  252.4 2.0 collective-permute-start.1
  256.1 5.3 %collective-permute-done.1 = f32[4,128,128]{2,1,0:T(8,128)S(1)} collective-permute-done((f32[4,128,128]{2,1,0:T(8,128)S(1)}, f32[4,128,128]{2,1,0:T(8,128)S(1)}, u32[]{:S(2)}, u32[]{:S(2)}) %collective-permute-start.1) | collective-permute-done | bytes 262176 | tf_op jit(solution)/shard_map/while/body/eval_jaxpr/ppermute | solution.py:16
  261.5 1.9 collective-permute-start
  263.6 3.4 collective-permute-start.1
  268.6 3.9 %collective-permute-done.1 = f32[4,128,128]{2,1,0:T(8,128)S(1)} collective-permute-done((f32[4,128,128]{2,1,0:T(8,128)S(1)}, f32[4,128,128]{2,1,0:T(8,128)S(1)}, u32[]{:S(2)}, u32[]{:S(2)}) %collective-permute-start.1) | collective-permute-done | bytes 262176 | tf_op jit(solution)/shard_map/while/body/eval_jaxpr/ppermute | solution.py:16
  272.7 6.0 %collective-permute-start = (f32[4,128,128]{2,1,0:T(8,128)S(1)}, f32[4,128,128]{2,1,0:T(8,128)S(1)}, u32[]{:S(2)}, u32[]{:S(2)}) collective-permute-start(f32[4,128,128]{2,1,0:T(8,128)S(1)} %multiply_add_fusion.7), channel_id=1, source_target_pairs={{0,2},{2,4},{4,6},{6,8},{8,10},{10,12},{12,14},{14,16},{16,18},{18... | collective-permute-start | bytes 786440 | tf_op jit(solution)/shard_map/while/body/eval_jaxpr/ppermute | solution.py:16
  278.7 1.9 collective-permute-start.1
  281.9 5.8 %collective-permute-done.1 = f32[4,128,128]{2,1,0:T(8,128)S(1)} collective-permute-done((f32[4,128,128]{2,1,0:T(8,128)S(1)}, f32[4,128,128]{2,1,0:T(8,128)S(1)}, u32[]{:S(2)}, u32[]{:S(2)}) %collective-permute-start.1) | collective-permute-done | bytes 262176 | tf_op jit(solution)/shard_map/while/body/eval_jaxpr/ppermute | solution.py:16
  287.8 2.4 collective-permute-start
  290.4 2.8 collective-permute-start.1
  293.2 2.3 collective-permute-done
  295.5 3.8 %collective-permute-done.1 = f32[4,128,128]{2,1,0:T(8,128)S(1)} collective-permute-done((f32[4,128,128]{2,1,0:T(8,128)S(1)}, f32[4,128,128]{2,1,0:T(8,128)S(1)}, u32[]{:S(2)}, u32[]{:S(2)}) %collective-permute-start.1) | collective-permute-done | bytes 262176 | tf_op jit(solution)/shard_map/while/body/eval_jaxpr/ppermute | solution.py:16
  299.4 13.1 %collective-permute-start = (f32[4,128,128]{2,1,0:T(8,128)S(1)}, f32[4,128,128]{2,1,0:T(8,128)S(1)}, u32[]{:S(2)}, u32[]{:S(2)}) collective-permute-start(f32[4,128,128]{2,1,0:T(8,128)S(1)} %multiply_add_fusion.7), channel_id=1, source_target_pairs={{0,2},{2,4},{4,6},{6,8},{8,10},{10,12},{12,14},{14,16},{16,18},{18... | collective-permute-start | bytes 786440 | tf_op jit(solution)/shard_map/while/body/eval_jaxpr/ppermute | solution.py:16
  312.7 1.9 collective-permute-start.1
  315.9 5.8 %collective-permute-done.1 = f32[4,128,128]{2,1,0:T(8,128)S(1)} collective-permute-done((f32[4,128,128]{2,1,0:T(8,128)S(1)}, f32[4,128,128]{2,1,0:T(8,128)S(1)}, u32[]{:S(2)}, u32[]{:S(2)}) %collective-permute-start.1) | collective-permute-done | bytes 262176 | tf_op jit(solution)/shard_map/while/body/eval_jaxpr/ppermute | solution.py:16
  321.8 4.4 %collective-permute-start = (f32[4,128,128]{2,1,0:T(8,128)S(1)}, f32[4,128,128]{2,1,0:T(8,128)S(1)}, u32[]{:S(2)}, u32[]{:S(2)}) collective-permute-start(f32[4,128,128]{2,1,0:T(8,128)S(1)} %multiply_add_fusion.7), channel_id=1, source_target_pairs={{0,2},{2,4},{4,6},{6,8},{8,10},{10,12},{12,14},{14,16},{16,18},{18... | collective-permute-start | bytes 786440 | tf_op jit(solution)/shard_map/while/body/eval_jaxpr/ppermute | solution.py:16
  326.3 1.9 collective-permute-start.1
  329.5 5.8 %collective-permute-done.1 = f32[4,128,128]{2,1,0:T(8,128)S(1)} collective-permute-done((f32[4,128,128]{2,1,0:T(8,128)S(1)}, f32[4,128,128]{2,1,0:T(8,128)S(1)}, u32[]{:S(2)}, u32[]{:S(2)}) %collective-permute-start.1) | collective-permute-done | bytes 262176 | tf_op jit(solution)/shard_map/while/body/eval_jaxpr/ppermute | solution.py:16
  335.3 2.3 multiply_bitcast_fusion
  337.6 2.0 fusion.57
  351.0 7.4 %reduce-scatter.2.cloned.1.call-done = f32[2,256,128]{2,1,0:T(8,128)} async-done(((f32[2,512,128]{2,1,0:T(8,128)}), f32[2,256,128]{2,1,0:T(8,128)}) %reduce-scatter.2.cloned.1.call-update) | async-done | bytes 262160 | tf_op jit(solution)/shard_map/reduce_scatter | solution.py:243
  (365 shorter events, 126.2 us)
Async XLA Ops:
  7.2 234.8 %copy-start = (bf16[512,4,128]{2,1,0:T(4,128)(2,1)S(1)}, bf16[512,4,128]{2,1,0:T(4,128)(2,1)}, u32[]{:S(2)}) copy-start(bf16[512,4,128]{2,1,0:T(4,128)(2,1)} %param.18) | copy-start | bytes 1572868
  7.2 7.9 %copy-start.12 = (bf16[512,4,128]{2,1,0:T(4,128)(2,1)S(1)}, bf16[512,4,128]{2,1,0:T(4,128)(2,1)}, u32[]{:S(2)}) copy-start(bf16[512,4,128]{2,1,0:T(4,128)(2,1)} %param.24) | copy-start | bytes 1572868
  7.2 351.2 %reduce-scatter.2.cloned.1.call-start = ((), (), s32[]{:S(2)}) async-start(), calls=%async_computation.1 | async-start | bytes 786432 | tf_op jit(solution)/shard_map/reduce_scatter | solution.py:243
  14.0 5.9 %copy-start.1 = (f32[512,512,4]{1,0,2:T(8,128)}, f32[512,512,4]{1,0,2:T(8,128)S(1)}, u32[]{:S(2)}) copy-start(f32[512,512,4]{1,0,2:T(8,128)S(1)} %get-tuple-element.908) | copy-start | bytes 12582916
  15.1 4.8 %copy-start.24 = (s32[32]{0:T(128)S(1)}, s32[32]{0:T(128)}, u32[]{:S(2)}) copy-start(s32[32]{0:T(128)} %param.25) | copy-start | bytes 388
  19.9 6.8 %collective-permute-start.2 = (bf16[512,128]{1,0:T(8,128)(2,1)S(1)}, bf16[512,128]{1,0:T(8,128)(2,1)S(1)}, u32[]{:S(2)}, u32[]{:S(2)}) collective-permute-start(bf16[512,128]{1,0:T(8,128)(2,1)S(1)} %get-tuple-element.1166), channel_id=1, source_target_pairs={{0,2},{2,4},{4,6},{6,8},{8,10},{10,12},{12,14},{14,16},{16,18},{18... | collective-permute-start | bytes 393224 | tf_op jit(solution)/shard_map/while/body/eval_jaxpr/ppermute | solution.py:16
  23.0 5.7 %collective-permute-start.3 = (bf16[512,128]{1,0:T(8,128)(2,1)S(1)}, bf16[512,128]{1,0:T(8,128)(2,1)S(1)}, u32[]{:S(2)}, u32[]{:S(2)}) collective-permute-start(bf16[512,128]{1,0:T(8,128)(2,1)S(1)} %get-tuple-element.1167), channel_id=1, source_target_pairs={{0,2},{2,4},{4,6},{6,8},{8,10},{10,12},{12,14},{14,16},{16,18},{18... | collective-permute-start | bytes 393224 | tf_op jit(solution)/shard_map/while/body/eval_jaxpr/ppermute | solution.py:16
  30.4 7.4 %collective-permute-start.2 = (bf16[512,128]{1,0:T(8,128)(2,1)S(1)}, bf16[512,128]{1,0:T(8,128)(2,1)S(1)}, u32[]{:S(2)}, u32[]{:S(2)}) collective-permute-start(bf16[512,128]{1,0:T(8,128)(2,1)S(1)} %get-tuple-element.1166), channel_id=1, source_target_pairs={{0,2},{2,4},{4,6},{6,8},{8,10},{10,12},{12,14},{14,16},{16,18},{18... | collective-permute-start | bytes 393224 | tf_op jit(solution)/shard_map/while/body/eval_jaxpr/ppermute | solution.py:16
  35.4 5.7 %collective-permute-start.3 = (bf16[512,128]{1,0:T(8,128)(2,1)S(1)}, bf16[512,128]{1,0:T(8,128)(2,1)S(1)}, u32[]{:S(2)}, u32[]{:S(2)}) collective-permute-start(bf16[512,128]{1,0:T(8,128)(2,1)S(1)} %get-tuple-element.1167), channel_id=1, source_target_pairs={{0,2},{2,4},{4,6},{6,8},{8,10},{10,12},{12,14},{14,16},{16,18},{18... | collective-permute-start | bytes 393224 | tf_op jit(solution)/shard_map/while/body/eval_jaxpr/ppermute | solution.py:16
  42.8 7.3 %collective-permute-start.2 = (bf16[512,128]{1,0:T(8,128)(2,1)S(1)}, bf16[512,128]{1,0:T(8,128)(2,1)S(1)}, u32[]{:S(2)}, u32[]{:S(2)}) collective-permute-start(bf16[512,128]{1,0:T(8,128)(2,1)S(1)} %get-tuple-element.1166), channel_id=1, source_target_pairs={{0,2},{2,4},{4,6},{6,8},{8,10},{10,12},{12,14},{14,16},{16,18},{18... | collective-permute-start | bytes 393224 | tf_op jit(solution)/shard_map/while/body/eval_jaxpr/ppermute | solution.py:16
  47.6 6.3 %collective-permute-start.3 = (bf16[512,128]{1,0:T(8,128)(2,1)S(1)}, bf16[512,128]{1,0:T(8,128)(2,1)S(1)}, u32[]{:S(2)}, u32[]{:S(2)}) collective-permute-start(bf16[512,128]{1,0:T(8,128)(2,1)S(1)} %get-tuple-element.1167), channel_id=1, source_target_pairs={{0,2},{2,4},{4,6},{6,8},{8,10},{10,12},{12,14},{14,16},{16,18},{18... | collective-permute-start | bytes 393224 | tf_op jit(solution)/shard_map/while/body/eval_jaxpr/ppermute | solution.py:16
  55.6 6.6 %collective-permute-start.2 = (bf16[512,128]{1,0:T(8,128)(2,1)S(1)}, bf16[512,128]{1,0:T(8,128)(2,1)S(1)}, u32[]{:S(2)}, u32[]{:S(2)}) collective-permute-start(bf16[512,128]{1,0:T(8,128)(2,1)S(1)} %get-tuple-element.1166), channel_id=1, source_target_pairs={{0,2},{2,4},{4,6},{6,8},{8,10},{10,12},{12,14},{14,16},{16,18},{18... | collective-permute-start | bytes 393224 | tf_op jit(solution)/shard_map/while/body/eval_jaxpr/ppermute | solution.py:16
  58.8 6.3 %collective-permute-start.3 = (bf16[512,128]{1,0:T(8,128)(2,1)S(1)}, bf16[512,128]{1,0:T(8,128)(2,1)S(1)}, u32[]{:S(2)}, u32[]{:S(2)}) collective-permute-start(bf16[512,128]{1,0:T(8,128)(2,1)S(1)} %get-tuple-element.1167), channel_id=1, source_target_pairs={{0,2},{2,4},{4,6},{6,8},{8,10},{10,12},{12,14},{14,16},{16,18},{18... | collective-permute-start | bytes 393224 | tf_op jit(solution)/shard_map/while/body/eval_jaxpr/ppermute | solution.py:16
  66.8 7.7 %collective-permute-start.2 = (bf16[512,128]{1,0:T(8,128)(2,1)S(1)}, bf16[512,128]{1,0:T(8,128)(2,1)S(1)}, u32[]{:S(2)}, u32[]{:S(2)}) collective-permute-start(bf16[512,128]{1,0:T(8,128)(2,1)S(1)} %get-tuple-element.1166), channel_id=1, source_target_pairs={{0,2},{2,4},{4,6},{6,8},{8,10},{10,12},{12,14},{14,16},{16,18},{18... | collective-permute-start | bytes 393224 | tf_op jit(solution)/shard_map/while/body/eval_jaxpr/ppermute | solution.py:16
  70.9 6.1 %collective-permute-start.3 = (bf16[512,128]{1,0:T(8,128)(2,1)S(1)}, bf16[512,128]{1,0:T(8,128)(2,1)S(1)}, u32[]{:S(2)}, u32[]{:S(2)}) collective-permute-start(bf16[512,128]{1,0:T(8,128)(2,1)S(1)} %get-tuple-element.1167), channel_id=1, source_target_pairs={{0,2},{2,4},{4,6},{6,8},{8,10},{10,12},{12,14},{14,16},{16,18},{18... | collective-permute-start | bytes 393224 | tf_op jit(solution)/shard_map/while/body/eval_jaxpr/ppermute | solution.py:16
  78.7 7.5 %collective-permute-start.2 = (bf16[512,128]{1,0:T(8,128)(2,1)S(1)}, bf16[512,128]{1,0:T(8,128)(2,1)S(1)}, u32[]{:S(2)}, u32[]{:S(2)}) collective-permute-start(bf16[512,128]{1,0:T(8,128)(2,1)S(1)} %get-tuple-element.1166), channel_id=1, source_target_pairs={{0,2},{2,4},{4,6},{6,8},{8,10},{10,12},{12,14},{14,16},{16,18},{18... | collective-permute-start | bytes 393224 | tf_op jit(solution)/shard_map/while/body/eval_jaxpr/ppermute | solution.py:16
  83.2 6.1 %collective-permute-start.3 = (bf16[512,128]{1,0:T(8,128)(2,1)S(1)}, bf16[512,128]{1,0:T(8,128)(2,1)S(1)}, u32[]{:S(2)}, u32[]{:S(2)}) collective-permute-start(bf16[512,128]{1,0:T(8,128)(2,1)S(1)} %get-tuple-element.1167), channel_id=1, source_target_pairs={{0,2},{2,4},{4,6},{6,8},{8,10},{10,12},{12,14},{14,16},{16,18},{18... | collective-permute-start | bytes 393224 | tf_op jit(solution)/shard_map/while/body/eval_jaxpr/ppermute | solution.py:16
  91.0 7.2 %copy-start.14 = (bf16[512,4,128]{2,0,1:T(8,128)(2,1)}, bf16[512,4,128]{2,0,1:T(8,128)(2,1)S(1)}, u32[]{:S(2)}) copy-start(bf16[512,4,128]{2,0,1:T(8,128)(2,1)S(1)} %get-tuple-element.1272) | copy-start | bytes 1572868
  91.0 7.1 %copy-start.16 = (f32[4,512]{1,0:T(4,128)}, f32[4,512]{1,0:T(4,128)S(1)}, u32[]{:S(2)}) copy-start(f32[4,512]{1,0:T(4,128)S(1)} %get-tuple-element.1210) | copy-start | bytes 24580
  100.5 134.2 %copy-start.13 = (bf16[512,4,128]{2,1,0:T(4,128)(2,1)S(1)}, bf16[512,4,128]{2,1,0:T(4,128)(2,1)}, u32[]{:S(2)}) copy-start(bf16[512,4,128]{2,1,0:T(4,128)(2,1)} %param.16) | copy-start | bytes 1572868
  100.5 8.3 %collective-permute-start.4 = (bf16[512,128]{1,0:T(8,128)(2,1)S(1)}, bf16[512,128]{1,0:T(8,128)(2,1)S(1)}, u32[]{:S(2)}, u32[]{:S(2)}) collective-permute-start(bf16[512,128]{1,0:T(8,128)(2,1)S(1)} %get-tuple-element.1222), channel_id=1, source_target_pairs={{0,2},{2,4},{4,6},{6,8},{8,10},{10,12},{12,14},{14,16},{16,18},{18... | collective-permute-start | bytes 393224 | tf_op jit(solution)/shard_map/while/body/eval_jaxpr/ppermute | solution.py:16
  104.5 5.9 %collective-permute-start.5 = (bf16[512,128]{1,0:T(8,128)(2,1)}, bf16[512,128]{1,0:T(8,128)(2,1)S(1)}, u32[]{:S(2)}, u32[]{:S(2)}) collective-permute-start(bf16[512,128]{1,0:T(8,128)(2,1)} %get-tuple-element.1223), channel_id=1, source_target_pairs={{0,2},{2,4},{4,6},{6,8},{8,10},{10,12},{12,14},{14,16},{16,18},{18... | collective-permute-start | bytes 393224 | tf_op jit(solution)/shard_map/while/body/eval_jaxpr/ppermute | solution.py:16
  106.4 12.7 %collective-permute-start.6 = (f32[2,512,128]{2,1,0:T(8,128)}, f32[2,512,128]{2,1,0:T(8,128)S(1)}, u32[]{:S(2)}, u32[]{:S(2)}) collective-permute-start(f32[2,512,128]{2,1,0:T(8,128)} %get-tuple-element.1224), channel_id=1, source_target_pairs={{0,2},{2,4},{4,6},{6,8},{8,10},{10,12},{12,14},{14,16},{16,18},{18... | collective-permute-start | bytes 1572872 | tf_op jit(solution)/shard_map/while/body/eval_jaxpr/ppermute | solution.py:26
  120.0 10.5 %collective-permute-start.4 = (bf16[512,128]{1,0:T(8,128)(2,1)S(1)}, bf16[512,128]{1,0:T(8,128)(2,1)S(1)}, u32[]{:S(2)}, u32[]{:S(2)}) collective-permute-start(bf16[512,128]{1,0:T(8,128)(2,1)S(1)} %get-tuple-element.1222), channel_id=1, source_target_pairs={{0,2},{2,4},{4,6},{6,8},{8,10},{10,12},{12,14},{14,16},{16,18},{18... | collective-permute-start | bytes 393224 | tf_op jit(solution)/shard_map/while/body/eval_jaxpr/ppermute | solution.py:16
  123.3 7.9 %collective-permute-start.5 = (bf16[512,128]{1,0:T(8,128)(2,1)}, bf16[512,128]{1,0:T(8,128)(2,1)S(1)}, u32[]{:S(2)}, u32[]{:S(2)}) collective-permute-start(bf16[512,128]{1,0:T(8,128)(2,1)} %get-tuple-element.1223), channel_id=1, source_target_pairs={{0,2},{2,4},{4,6},{6,8},{8,10},{10,12},{12,14},{14,16},{16,18},{18... | collective-permute-start | bytes 393224 | tf_op jit(solution)/shard_map/while/body/eval_jaxpr/ppermute | solution.py:16
  126.3 14.5 %collective-permute-start.6 = (f32[2,512,128]{2,1,0:T(8,128)}, f32[2,512,128]{2,1,0:T(8,128)S(1)}, u32[]{:S(2)}, u32[]{:S(2)}) collective-permute-start(f32[2,512,128]{2,1,0:T(8,128)} %get-tuple-element.1224), channel_id=1, source_target_pairs={{0,2},{2,4},{4,6},{6,8},{8,10},{10,12},{12,14},{14,16},{16,18},{18... | collective-permute-start | bytes 1572872 | tf_op jit(solution)/shard_map/while/body/eval_jaxpr/ppermute | solution.py:26
  141.7 9.0 %collective-permute-start.4 = (bf16[512,128]{1,0:T(8,128)(2,1)S(1)}, bf16[512,128]{1,0:T(8,128)(2,1)S(1)}, u32[]{:S(2)}, u32[]{:S(2)}) collective-permute-start(bf16[512,128]{1,0:T(8,128)(2,1)S(1)} %get-tuple-element.1222), channel_id=1, source_target_pairs={{0,2},{2,4},{4,6},{6,8},{8,10},{10,12},{12,14},{14,16},{16,18},{18... | collective-permute-start | bytes 393224 | tf_op jit(solution)/shard_map/while/body/eval_jaxpr/ppermute | solution.py:16
  147.5 5.9 %collective-permute-start.5 = (bf16[512,128]{1,0:T(8,128)(2,1)}, bf16[512,128]{1,0:T(8,128)(2,1)S(1)}, u32[]{:S(2)}, u32[]{:S(2)}) collective-permute-start(bf16[512,128]{1,0:T(8,128)(2,1)} %get-tuple-element.1223), channel_id=1, source_target_pairs={{0,2},{2,4},{4,6},{6,8},{8,10},{10,12},{12,14},{14,16},{16,18},{18... | collective-permute-start | bytes 393224 | tf_op jit(solution)/shard_map/while/body/eval_jaxpr/ppermute | solution.py:16
  149.4 12.7 %collective-permute-start.6 = (f32[2,512,128]{2,1,0:T(8,128)}, f32[2,512,128]{2,1,0:T(8,128)S(1)}, u32[]{:S(2)}, u32[]{:S(2)}) collective-permute-start(f32[2,512,128]{2,1,0:T(8,128)} %get-tuple-element.1224), channel_id=1, source_target_pairs={{0,2},{2,4},{4,6},{6,8},{8,10},{10,12},{12,14},{14,16},{16,18},{18... | collective-permute-start | bytes 1572872 | tf_op jit(solution)/shard_map/while/body/eval_jaxpr/ppermute | solution.py:26
  162.9 9.0 %collective-permute-start.4 = (bf16[512,128]{1,0:T(8,128)(2,1)S(1)}, bf16[512,128]{1,0:T(8,128)(2,1)S(1)}, u32[]{:S(2)}, u32[]{:S(2)}) collective-permute-start(bf16[512,128]{1,0:T(8,128)(2,1)S(1)} %get-tuple-element.1222), channel_id=1, source_target_pairs={{0,2},{2,4},{4,6},{6,8},{8,10},{10,12},{12,14},{14,16},{16,18},{18... | collective-permute-start | bytes 393224 | tf_op jit(solution)/shard_map/while/body/eval_jaxpr/ppermute | solution.py:16
  168.7 6.4 %collective-permute-start.5 = (bf16[512,128]{1,0:T(8,128)(2,1)}, bf16[512,128]{1,0:T(8,128)(2,1)S(1)}, u32[]{:S(2)}, u32[]{:S(2)}) collective-permute-start(bf16[512,128]{1,0:T(8,128)(2,1)} %get-tuple-element.1223), channel_id=1, source_target_pairs={{0,2},{2,4},{4,6},{6,8},{8,10},{10,12},{12,14},{14,16},{16,18},{18... | collective-permute-start | bytes 393224 | tf_op jit(solution)/shard_map/while/body/eval_jaxpr/ppermute | solution.py:16
  170.7 13.2 %collective-permute-start.6 = (f32[2,512,128]{2,1,0:T(8,128)}, f32[2,512,128]{2,1,0:T(8,128)S(1)}, u32[]{:S(2)}, u32[]{:S(2)}) collective-permute-start(f32[2,512,128]{2,1,0:T(8,128)} %get-tuple-element.1224), channel_id=1, source_target_pairs={{0,2},{2,4},{4,6},{6,8},{8,10},{10,12},{12,14},{14,16},{16,18},{18... | collective-permute-start | bytes 1572872 | tf_op jit(solution)/shard_map/while/body/eval_jaxpr/ppermute | solution.py:26
  184.7 8.7 %collective-permute-start.4 = (bf16[512,128]{1,0:T(8,128)(2,1)S(1)}, bf16[512,128]{1,0:T(8,128)(2,1)S(1)}, u32[]{:S(2)}, u32[]{:S(2)}) collective-permute-start(bf16[512,128]{1,0:T(8,128)(2,1)S(1)} %get-tuple-element.1222), channel_id=1, source_target_pairs={{0,2},{2,4},{4,6},{6,8},{8,10},{10,12},{12,14},{14,16},{16,18},{18... | collective-permute-start | bytes 393224 | tf_op jit(solution)/shard_map/while/body/eval_jaxpr/ppermute | solution.py:16
  189.8 7.2 %collective-permute-start.5 = (bf16[512,128]{1,0:T(8,128)(2,1)}, bf16[512,128]{1,0:T(8,128)(2,1)S(1)}, u32[]{:S(2)}, u32[]{:S(2)}) collective-permute-start(bf16[512,128]{1,0:T(8,128)(2,1)} %get-tuple-element.1223), channel_id=1, source_target_pairs={{0,2},{2,4},{4,6},{6,8},{8,10},{10,12},{12,14},{14,16},{16,18},{18... | collective-permute-start | bytes 393224 | tf_op jit(solution)/shard_map/while/body/eval_jaxpr/ppermute | solution.py:16
  191.7 14.4 %collective-permute-start.6 = (f32[2,512,128]{2,1,0:T(8,128)}, f32[2,512,128]{2,1,0:T(8,128)S(1)}, u32[]{:S(2)}, u32[]{:S(2)}) collective-permute-start(f32[2,512,128]{2,1,0:T(8,128)} %get-tuple-element.1224), channel_id=1, source_target_pairs={{0,2},{2,4},{4,6},{6,8},{8,10},{10,12},{12,14},{14,16},{16,18},{18... | collective-permute-start | bytes 1572872 | tf_op jit(solution)/shard_map/while/body/eval_jaxpr/ppermute | solution.py:26
  193.1 4.0 %copy-start.15 = (bf16[512,4,128]{2,0,1:T(8,128)(2,1)S(1)}, bf16[512,4,128]{2,0,1:T(8,128)(2,1)}, u32[]{:S(2)}) copy-start(bf16[512,4,128]{2,0,1:T(8,128)(2,1)} %get-tuple-element.1249) | copy-start | bytes 1572868 | tf_op jit(solution)/shard_map/while
  193.1 4.0 %copy-start.17 = (f32[4,512]{1,0:T(4,128)S(1)}, f32[4,512]{1,0:T(4,128)}, u32[]{:S(2)}) copy-start(f32[4,512]{1,0:T(4,128)} %get-tuple-element.1250) | copy-start | bytes 24580 | tf_op jit(solution)/shard_map/while
  207.0 7.7 %collective-permute-start.4 = (bf16[512,128]{1,0:T(8,128)(2,1)S(1)}, bf16[512,128]{1,0:T(8,128)(2,1)S(1)}, u32[]{:S(2)}, u32[]{:S(2)}) collective-permute-start(bf16[512,128]{1,0:T(8,128)(2,1)S(1)} %get-tuple-element.1222), channel_id=1, source_target_pairs={{0,2},{2,4},{4,6},{6,8},{8,10},{10,12},{12,14},{14,16},{16,18},{18... | collective-permute-start | bytes 393224 | tf_op jit(solution)/shard_map/while/body/eval_jaxpr/ppermute | solution.py:16
  210.7 7.0 %collective-permute-start.5 = (bf16[512,128]{1,0:T(8,128)(2,1)}, bf16[512,128]{1,0:T(8,128)(2,1)S(1)}, u32[]{:S(2)}, u32[]{:S(2)}) collective-permute-start(bf16[512,128]{1,0:T(8,128)(2,1)} %get-tuple-element.1223), channel_id=1, source_target_pairs={{0,2},{2,4},{4,6},{6,8},{8,10},{10,12},{12,14},{14,16},{16,18},{18... | collective-permute-start | bytes 393224 | tf_op jit(solution)/shard_map/while/body/eval_jaxpr/ppermute | solution.py:16
  212.6 14.6 %collective-permute-start.6 = (f32[2,512,128]{2,1,0:T(8,128)}, f32[2,512,128]{2,1,0:T(8,128)S(1)}, u32[]{:S(2)}, u32[]{:S(2)}) collective-permute-start(f32[2,512,128]{2,1,0:T(8,128)} %get-tuple-element.1224), channel_id=1, source_target_pairs={{0,2},{2,4},{4,6},{6,8},{8,10},{10,12},{12,14},{14,16},{16,18},{18... | collective-permute-start | bytes 1572872 | tf_op jit(solution)/shard_map/while/body/eval_jaxpr/ppermute | solution.py:26
  228.1 115.3 %collective-permute-start.7 = (f32[2,512,128]{2,1,0:T(8,128)}, f32[2,512,128]{2,1,0:T(8,128)}, u32[]{:S(2)}, u32[]{:S(2)}) collective-permute-start(f32[2,512,128]{2,1,0:T(8,128)} %get-tuple-element.693), channel_id=1, source_target_pairs={{0,20},{2,22},{4,24},{6,26},{8,28},{10,30},{12,0},{14,2},{16,4},{1... | collective-permute-start | bytes 1572872 | tf_op jit(solution)/shard_map/ppermute | solution.py:26
  234.0 7.9 %copy-start.20 = (f32[2,4]{1,0:T(2,128)}, f32[2,4]{1,0:T(2,128)S(1)}, u32[]{:S(2)}) copy-start(f32[2,4]{1,0:T(2,128)S(1)} %get-tuple-element.900) | copy-start | bytes 100
  234.8 7.2 %copy-start.7 = (bf16[512,4,128]{2,0,1:T(8,128)(2,1)}, bf16[512,4,128]{2,0,1:T(8,128)(2,1)S(1)}, u32[]{:S(2)}) copy-start(bf16[512,4,128]{2,0,1:T(8,128)(2,1)S(1)} %copy.58) | copy-start | bytes 1572868
  236.1 8.7 %copy-start.3 = (bf16[512,4,128]{2,0,1:T(8,128)(2,1)}, bf16[512,4,128]{2,0,1:T(8,128)(2,1)S(1)}, u32[]{:S(2)}) copy-start(bf16[512,4,128]{2,0,1:T(8,128)(2,1)S(1)} %copy.52) | copy-start | bytes 1572868
  238.7 8.7 %copy-start.11 = (f32[2,4,128,128]{3,2,1,0:T(8,128)}, f32[2,4,128,128]{3,2,1,0:T(8,128)S(1)}, u32[]{:S(2)}) copy-start(f32[2,4,128,128]{3,2,1,0:T(8,128)S(1)} %fusion.62) | copy-start | bytes 1572868
  242.0 5.4 %copy-start.22 = (f32[4]{0:T(128)S(1)}, f32[4]{0:T(128)}, u32[]{:S(2)}) copy-start(f32[4]{0:T(128)} %get-tuple-element.896) | copy-start | bytes 52
  242.0 6.1 %copy-start.23 = (f32[4]{0:T(128)S(1)}, f32[4]{0:T(128)}, u32[]{:S(2)}) copy-start(f32[4]{0:T(128)} %get-tuple-element.897) | copy-start | bytes 52
  242.0 5.3 %copy-start.21 = (f32[2,4]{1,0:T(2,128)S(1)}, f32[2,4]{1,0:T(2,128)}, u32[]{:S(2)}) copy-start(f32[2,4]{1,0:T(2,128)} %copy-done.20) | copy-start | bytes 100
  242.0 6.9 %copy-start.18 = (f32[4]{0:T(128)S(1)}, f32[4]{0:T(128)}, u32[]{:S(2)}) copy-start(f32[4]{0:T(128)} %get-tuple-element.1124) | copy-start | bytes 52
  242.0 6.9 %copy-start.19 = (f32[4]{0:T(128)S(1)}, f32[4]{0:T(128)}, u32[]{:S(2)}) copy-start(f32[4]{0:T(128)} %get-tuple-element.1122) | copy-start | bytes 52
  249.0 7.1 %collective-permute-start = (f32[4,128,128]{2,1,0:T(8,128)S(1)}, f32[4,128,128]{2,1,0:T(8,128)S(1)}, u32[]{:S(2)}, u32[]{:S(2)}) collective-permute-start(f32[4,128,128]{2,1,0:T(8,128)S(1)} %multiply_add_fusion.7), channel_id=1, source_target_pairs={{0,2},{2,4},{4,6},{6,8},{8,10},{10,12},{12,14},{14,16},{16,18},{18... | collective-permute-start | bytes 786440 | tf_op jit(solution)/shard_map/while/body/eval_jaxpr/ppermute | solution.py:16
  252.4 9.0 %collective-permute-start.1 = (f32[4,128,128]{2,1,0:T(8,128)S(1)}, f32[4,128,128]{2,1,0:T(8,128)S(1)}, u32[]{:S(2)}, u32[]{:S(2)}) collective-permute-start(f32[4,128,128]{2,1,0:T(8,128)S(1)} %multiply_add_fusion.8), channel_id=1, source_target_pairs={{2,0},{4,2},{6,4},{8,6},{10,8},{12,10},{14,12},{16,14},{18,16},{20... | collective-permute-start | bytes 786440 | tf_op jit(solution)/shard_map/while/body/eval_jaxpr/ppermute | solution.py:16
  261.5 7.1 %collective-permute-start = (f32[4,128,128]{2,1,0:T(8,128)S(1)}, f32[4,128,128]{2,1,0:T(8,128)S(1)}, u32[]{:S(2)}, u32[]{:S(2)}) collective-permute-start(f32[4,128,128]{2,1,0:T(8,128)S(1)} %multiply_add_fusion.7), channel_id=1, source_target_pairs={{0,2},{2,4},{4,6},{6,8},{8,10},{10,12},{12,14},{14,16},{16,18},{18... | collective-permute-start | bytes 786440 | tf_op jit(solution)/shard_map/while/body/eval_jaxpr/ppermute | solution.py:16
  263.6 9.0 %collective-permute-start.1 = (f32[4,128,128]{2,1,0:T(8,128)S(1)}, f32[4,128,128]{2,1,0:T(8,128)S(1)}, u32[]{:S(2)}, u32[]{:S(2)}) collective-permute-start(f32[4,128,128]{2,1,0:T(8,128)S(1)} %multiply_add_fusion.8), channel_id=1, source_target_pairs={{2,0},{4,2},{6,4},{8,6},{10,8},{12,10},{14,12},{16,14},{18,16},{20... | collective-permute-start | bytes 786440 | tf_op jit(solution)/shard_map/while/body/eval_jaxpr/ppermute | solution.py:16
  272.7 9.3 %collective-permute-start = (f32[4,128,128]{2,1,0:T(8,128)S(1)}, f32[4,128,128]{2,1,0:T(8,128)S(1)}, u32[]{:S(2)}, u32[]{:S(2)}) collective-permute-start(f32[4,128,128]{2,1,0:T(8,128)S(1)} %multiply_add_fusion.7), channel_id=1, source_target_pairs={{0,2},{2,4},{4,6},{6,8},{8,10},{10,12},{12,14},{14,16},{16,18},{18... | collective-permute-start | bytes 786440 | tf_op jit(solution)/shard_map/while/body/eval_jaxpr/ppermute | solution.py:16
  278.7 9.0 %collective-permute-start.1 = (f32[4,128,128]{2,1,0:T(8,128)S(1)}, f32[4,128,128]{2,1,0:T(8,128)S(1)}, u32[]{:S(2)}, u32[]{:S(2)}) collective-permute-start(f32[4,128,128]{2,1,0:T(8,128)S(1)} %multiply_add_fusion.8), channel_id=1, source_target_pairs={{2,0},{4,2},{6,4},{8,6},{10,8},{12,10},{14,12},{16,14},{18,16},{20... | collective-permute-start | bytes 786440 | tf_op jit(solution)/shard_map/while/body/eval_jaxpr/ppermute | solution.py:16
  287.8 7.7 %collective-permute-start = (f32[4,128,128]{2,1,0:T(8,128)S(1)}, f32[4,128,128]{2,1,0:T(8,128)S(1)}, u32[]{:S(2)}, u32[]{:S(2)}) collective-permute-start(f32[4,128,128]{2,1,0:T(8,128)S(1)} %multiply_add_fusion.7), channel_id=1, source_target_pairs={{0,2},{2,4},{4,6},{6,8},{8,10},{10,12},{12,14},{14,16},{16,18},{18... | collective-permute-start | bytes 786440 | tf_op jit(solution)/shard_map/while/body/eval_jaxpr/ppermute | solution.py:16
  290.4 8.9 %collective-permute-start.1 = (f32[4,128,128]{2,1,0:T(8,128)S(1)}, f32[4,128,128]{2,1,0:T(8,128)S(1)}, u32[]{:S(2)}, u32[]{:S(2)}) collective-permute-start(f32[4,128,128]{2,1,0:T(8,128)S(1)} %multiply_add_fusion.8), channel_id=1, source_target_pairs={{2,0},{4,2},{6,4},{8,6},{10,8},{12,10},{14,12},{16,14},{18,16},{20... | collective-permute-start | bytes 786440 | tf_op jit(solution)/shard_map/while/body/eval_jaxpr/ppermute | solution.py:16
  299.4 16.4 %collective-permute-start = (f32[4,128,128]{2,1,0:T(8,128)S(1)}, f32[4,128,128]{2,1,0:T(8,128)S(1)}, u32[]{:S(2)}, u32[]{:S(2)}) collective-permute-start(f32[4,128,128]{2,1,0:T(8,128)S(1)} %multiply_add_fusion.7), channel_id=1, source_target_pairs={{0,2},{2,4},{4,6},{6,8},{8,10},{10,12},{12,14},{14,16},{16,18},{18... | collective-permute-start | bytes 786440 | tf_op jit(solution)/shard_map/while/body/eval_jaxpr/ppermute | solution.py:16
  312.7 9.0 %collective-permute-start.1 = (f32[4,128,128]{2,1,0:T(8,128)S(1)}, f32[4,128,128]{2,1,0:T(8,128)S(1)}, u32[]{:S(2)}, u32[]{:S(2)}) collective-permute-start(f32[4,128,128]{2,1,0:T(8,128)S(1)} %multiply_add_fusion.8), channel_id=1, source_target_pairs={{2,0},{4,2},{6,4},{8,6},{10,8},{12,10},{14,12},{16,14},{18,16},{20... | collective-permute-start | bytes 786440 | tf_op jit(solution)/shard_map/while/body/eval_jaxpr/ppermute | solution.py:16
  321.8 7.7 %collective-permute-start = (f32[4,128,128]{2,1,0:T(8,128)S(1)}, f32[4,128,128]{2,1,0:T(8,128)S(1)}, u32[]{:S(2)}, u32[]{:S(2)}) collective-permute-start(f32[4,128,128]{2,1,0:T(8,128)S(1)} %multiply_add_fusion.7), channel_id=1, source_target_pairs={{0,2},{2,4},{4,6},{6,8},{8,10},{10,12},{12,14},{14,16},{16,18},{18... | collective-permute-start | bytes 786440 | tf_op jit(solution)/shard_map/while/body/eval_jaxpr/ppermute | solution.py:16
  326.3 9.0 %collective-permute-start.1 = (f32[4,128,128]{2,1,0:T(8,128)S(1)}, f32[4,128,128]{2,1,0:T(8,128)S(1)}, u32[]{:S(2)}, u32[]{:S(2)}) collective-permute-start(f32[4,128,128]{2,1,0:T(8,128)S(1)} %multiply_add_fusion.8), channel_id=1, source_target_pairs={{2,0},{4,2},{6,4},{8,6},{10,8},{12,10},{14,12},{16,14},{18,16},{20... | collective-permute-start | bytes 786440 | tf_op jit(solution)/shard_map/while/body/eval_jaxpr/ppermute | solution.py:16
  335.3 5.6 %copy-start.5 = (bf16[2,4,256,256]{3,2,1,0:T(8,128)(2,1)S(1)}, bf16[2,4,256,256]{3,2,1,0:T(8,128)(2,1)}, u32[]{:S(2)}) copy-start(bf16[2,4,256,256]{3,2,1,0:T(8,128)(2,1)} %multiply_convert_fusion.1) | copy-start | bytes 3145732
  335.3 5.6 %copy-start.8 = (bf16[512,4,128]{2,0,1:T(8,128)(2,1)S(1)}, bf16[512,4,128]{2,0,1:T(8,128)(2,1)}, u32[]{:S(2)}) copy-start(bf16[512,4,128]{2,0,1:T(8,128)(2,1)} %copy-done.7) | copy-start | bytes 1572868
  (15 other events, 42.5 us)
Sparse Core Ops, SparseCore 0:
  343.5 14.8 reduce-scatter.1
where the time goes:
time: 371 us; the launch traced here: 368 us
  starting transfers between devices  131 us (35%)
  waiting for transfers between devices  89.4 us (24%)
  matrix products  71.5 us (19%)
  other arithmetic  33.1 us (9%)
  local copies, waits for them, and re-layouts  26.1 us (7%)
  between operations  15.7 us (4%)
    ppermute x36, starting transfers between devices, shifted(): lax.ppermute(value, axis, [(source, source + steps) for source in range(f...  125 us
    ppermute x36, waiting for transfers between devices, shifted(): lax.ppermute(value, axis, [(source, source + steps) for source in range(f...  56.5 us
    ppermute x7, waiting for transfers between devices, shifted_2(): return lax.ppermute(value, axis, pairs)  25.5 us
    dot_general x7, matrix products, gather_stats(): jnp.einsum('thd,sd->hts', att_dout, values, preferred_element_type=jnp.fl...  14.4 us
    unnamed x60, local copies, waits for them, and re-layouts  10.3 us
    dot_general x6, matrix products, grad_terms(): jnp.einsum('thd,sd->hts', att_dout, values, preferred_element_type=jnp.fl...  9.21 us
    dot_general x7, matrix products, grad_terms(): jnp.einsum('hts,thd->sd', probs_b, att_dout, preferred_element_type=jnp.f...  8.75 us
  transfers between devices with their start and end apart: 44, of which 30 were waited for; matrix products, arithmetic and copies ran while one was open for 24% of the time, Pallas kernels for 0%

commit v1 on v0

v1 whole, which is shorter than its diff:
```python
import functools
import math

import jax
import jax.numpy as jnp
from jax import lax
from jax.experimental import pallas as pl
from jax.experimental.pallas import tpu as pltpu
from jax.sharding import PartitionSpec as P

TILE = 256
MOST = 12
NEG = -1e30
MESH = pl.DeviceIdType.MESH
F32 = jnp.float32
BF16 = jnp.bfloat16


def dot_nn(a, b):
    return lax.dot_general(a, b, (((1,), (0,)), ((), ())), preferred_element_type=F32)


def dot_nt(a, b):
    return lax.dot_general(a, b, (((1,), (1,)), ((), ())), preferred_element_type=F32)


def dot_tn(a, b):
    return lax.dot_general(a, b, (((0,), (0,)), ((), ())), preferred_element_type=F32)


def split(x):
    high = x.astype(BF16)
    return high, (x - high.astype(F32)).astype(BF16)


def greet(me, core, count, reach):
    barrier = pltpu.get_barrier_semaphore()
    pl.semaphore_signal(barrier, inc=1, device_id={"head": 1 - core}, device_id_type=MESH)
    for step in range(1, reach + 1):

        @pl.when(me + step < count)
        def _():
            pl.semaphore_signal(barrier, inc=1, device_id={"ctx": me + step}, device_id_type=MESH)

        @pl.when(me - step >= 0)
        def _():
            pl.semaphore_signal(barrier, inc=1, device_id={"ctx": me - step}, device_id_type=MESH)

    pl.semaphore_wait(
        barrier, 1 + jnp.minimum(me, reach) + jnp.minimum(count - 1 - me, reach)
    )


def lightning_kernel(
    count, reach, heads, nblocks,
    doc, lq, lk, lv, ld, dec, att_k, att_v,
    dq, dk, dv, kall, vall,
    wide, parts, grads, states,
    send_l, recv_l, send_r, recv_r, echo_l, land_l, echo_r, land_r,
    own_sem, kv_send, kv_recv, pair_send, pair_recv, st_send, st_recv,
):
    me = lax.axis_index("ctx")
    core = lax.axis_index("head")
    length = nblocks * TILE
    half = length // 2
    width = lq.shape[1]
    rows = TILE * heads
    greet(me, core, count, reach)

    pairs = ((att_k, kall), (att_v, vall))
    start = pl.multiple_of(core * half, half)

    def kv_copy(which, step):
        source, target = pairs[which]
        place = pl.multiple_of((reach - step) * length + core * half, half)
        return pltpu.make_async_remote_copy(
            src_ref=source.at[pl.ds(start, half)],
            dst_ref=target.at[pl.ds(place, half)],
            send_sem=kv_send.at[which, step - 1],
            recv_sem=kv_recv.at[which, step - 1],
            device_id={"ctx": me + step},
            device_id_type=MESH,
        )

    def pair_copy(which, step):
        target = pairs[which][1]
        place = pl.multiple_of((reach - step) * length + core * half, half)
        return pltpu.make_async_remote_copy(
            src_ref=target.at[pl.ds(place, half)],
            dst_ref=target.at[pl.ds(place, half)],
            send_sem=pair_send.at[which, step - 1],
            recv_sem=pair_recv.at[which, step - 1],
            device_id={"head": 1 - core},
            device_id_type=MESH,
        )

    for step in range(1, reach + 1):

        @pl.when(me + step < count)
        def _():
            kv_copy(0, step).start()
            kv_copy(1, step).start()

    own = [
        pltpu.make_async_copy(
            pairs[which][0], pairs[which][1].at[pl.ds(reach * length, length)], own_sem.at[which]
        )
        for which in range(2)
    ]
    own[0].start()
    own[1].start()

    t_sub = lax.broadcasted_iota(jnp.int32, (TILE, TILE), 0)
    t_lane = lax.broadcasted_iota(jnp.int32, (TILE, TILE), 1)
    upper = (t_sub <= t_lane).astype(F32)
    lower = (t_sub >= t_lane).astype(F32)

    def link(at_one, at_two):
        one = jnp.clip(at_one, 0, count * nblocks - 1)
        two = jnp.clip(at_two, 0, count * nblocks - 1)
        inside = jnp.logical_and(at_one >= 0, at_two < count * nblocks)
        same = jnp.logical_and(doc[one] == doc[two], inside)
        return jnp.where(same, 1.0, 0.0).astype(F32)

    follows = [link(me * nblocks + b - 1, me * nblocks + b) for b in range(nblocks)]
    precedes = [link(me * nblocks + b, me * nblocks + b + 1) for b in range(nblocks)]

    cum_row, cum_col = [], []
    for b in range(nblocks):
        piece = dec[:, b * TILE : (b + 1) * TILE]
        cum_row.append(
            lax.dot_general(
                piece, upper, (((1,), (0,)), ((), ())),
                preferred_element_type=F32, precision=lax.Precision.HIGHEST,
            )
        )
        cum_col.append(
            lax.dot_general(
                lower, piece, (((1,), (1,)), ((), ())),
                preferred_element_type=F32, precision=lax.Precision.HIGHEST,
            )
        )

    def head_terms(b, h):
        row = cum_row[b][h : h + 1, :]
        col = cum_col[b][:, h : h + 1]
        total = col[TILE - 1 : TILE, :]
        return row, col, total

    for b in range(nblocks):
        for a, ref in enumerate((lq, lk, lv, ld)):
            wide[a] = ref[b * rows : (b + 1) * rows, :].astype(F32)
        for h in range(heads):
            row, col, total = head_terms(b, h)
            picked = [wide[a, pl.ds(h, TILE, stride=heads), :] for a in range(4)]
            for a in range(4):
                parts[a, b, h] = picked[a].astype(BF16)
            key_high, key_low = split((picked[1] * jnp.exp(total - col)).T)
            value = picked[2].astype(BF16)
            states[0, b, h] = dot_nn(key_high, value) + dot_nn(key_low, value)
            query_high, query_low = split((picked[0] * jnp.exp(col)).T)
            dout = picked[3].astype(BF16)
            states[1, b, h] = dot_nn(query_high, dout) + dot_nn(query_low, dout)

    for h in range(heads):
        keep = [jnp.exp(head_terms(b, h)[2]) for b in range(nblocks)]
        total_l = states[0, 0, h]
        mult_l = keep[0] * follows[0]
        for b in range(1, nblocks):
            total_l = states[0, b, h] + keep[b] * follows[b] * total_l
            mult_l = mult_l * keep[b] * follows[b]
        total_r = states[1, nblocks - 1, h]
        mult_r = keep[nblocks - 1] * precedes[nblocks - 1]
        for b in reversed(range(nblocks - 1)):
            total_r = states[1, b, h] + keep[b] * precedes[b] * total_r
            mult_r = mult_r * keep[b] * precedes[b]
        send_l[h, 0:width, :] = total_l
        send_r[h, 0:width, :] = total_r
        send_l[h, width : width + 8, :] = jnp.broadcast_to(mult_l, (8, width))
        send_r[h, width : width + 8, :] = jnp.broadcast_to(mult_r, (8, width))

    def state_copy(side, step):
        return pltpu.make_async_remote_copy(
            src_ref=(send_l, send_r)[side],
            dst_ref=(recv_l, recv_r)[side].at[step - 1],
            send_sem=st_send.at[side, step - 1],
            recv_sem=st_recv.at[side, step - 1],
            device_id={"ctx": me + step if side == 0 else me - step},
            device_id_type=MESH,
        )

    def echo_copy(side):
        return pltpu.make_async_remote_copy(
            src_ref=(echo_l, echo_r)[side],
            dst_ref=(land_l, land_r)[side],
            send_sem=st_send.at[side, 3],
            recv_sem=st_recv.at[side, 3],
            device_id={"ctx": me + 3 if side == 0 else me - 3},
            device_id_type=MESH,
        )

    for step in (1, 2, 3):

        @pl.when(me + step < count)
        def _():
            state_copy(0, step).start()

        @pl.when(me - step >= 0)
        def _():
            state_copy(1, step).start()

        @pl.when(me - step < 0)
        def _():
            recv_l[step - 1] = jnp.zeros(recv_l.shape[1:], F32)

        @pl.when(me + step >= count)
        def _():
            recv_r[step - 1] = jnp.zeros(recv_r.shape[1:], F32)

    @pl.when(me - 3 < 0)
    def _():
        land_l[...] = jnp.zeros(land_l.shape, F32)

    @pl.when(me + 3 >= count)
    def _():
        land_r[...] = jnp.zeros(land_r.shape, F32)

    def within(b):
        for h in range(heads):
            row, col, total = head_terms(b, h)
            query, key, value, dout = (parts[a, b, h] for a in range(4))
            seen = t_sub <= t_lane
            weight = jnp.where(seen, jnp.exp(jnp.where(seen, row - col, 0.0)), 0.0)
            left = (dot_nt(value, dout) * weight).astype(BF16)
            right = (dot_nt(key, query) * weight).astype(BF16)
            at = pl.ds(b * rows + h, TILE, stride=heads)
            grads[0, at, :] = dot_tn(left, key)
            grads[1, at, :] = dot_nn(left, query)
            grads[2, at, :] = dot_nn(right, dout)

    for b in range(nblocks):
        within(b)

    def wait_states(step):
        @pl.when(me - step >= 0)
        def _():
            state_copy(0, step).wait_recv()

        @pl.when(me + step < count)
        def _():
            state_copy(1, step).wait_recv()

    for step in (1, 2, 3):
        wait_states(step)
    for recv, echo in ((recv_l, echo_l), (recv_r, echo_r)):
        for h in range(heads):
            one = recv[0, h, width : width + 1, :]
            two = recv[1, h, width : width + 1, :]
            echo[h] = recv[0, h, 0:width, :] + one * (
                recv[1, h, 0:width, :] + two * recv[2, h, 0:width, :]
            )

    @pl.when(me + 3 < count)
    def _():
        echo_copy(0).start()

    @pl.when(me - 3 >= 0)
    def _():
        echo_copy(1).start()

    def pass_on(step):
        @pl.when(me - step >= 0)
        def _():
            for which in range(2):
                kv_copy(which, step).wait_recv()
                pair_copy(which, step).start()

    pass_on(1)
    pass_on(2)

    @pl.when(me - 3 >= 0)
    def _():
        echo_copy(0).wait_recv()

    @pl.when(me + 3 < count)
    def _():
        echo_copy(1).wait_recv()

    for h in range(heads):
        keep = [jnp.exp(head_terms(b, h)[2]) for b in range(nblocks)]
        span_l = recv_l[0, h, width : width + 1, :] * recv_l[1, h, width : width + 1, :]
        span_l = span_l * recv_l[2, h, width : width + 1, :]
        span_r = recv_r[0, h, width : width + 1, :] * recv_r[1, h, width : width + 1, :]
        span_r = span_r * recv_r[2, h, width : width + 1, :]
        state = echo_l[h] + span_l * land_l[h]
        into = []
        for b in range(nblocks):
            into.append(follows[b] * state)
            state = states[0, b, h] + keep[b] * into[b]
        state = echo_r[h] + span_r * land_r[h]
        back = [None] * nblocks
        for b in reversed(range(nblocks)):
            back[b] = precedes[b] * state
            state = states[1, b, h] + keep[b] * back[b]
        for b in range(nblocks):
            row, col, total = head_terms(b, h)
            query, key, value, dout = (parts[a, b, h] for a in range(4))
            head_decay = jnp.exp(col)
            tail_decay = jnp.exp(total - col)
            into_high, into_low = split(into[b])
            back_high, back_low = split(back[b])
            at = pl.ds(b * rows + h, TILE, stride=heads)
            grads[0, at, :] = grads[0, at, :] + head_decay * (
                dot_nt(dout, into_high) + dot_nt(dout, into_low)
            )
            grads[1, at, :] = grads[1, at, :] + tail_decay * (
                dot_nt(value, back_high) + dot_nt(value, back_low)
            )
            grads[2, at, :] = grads[2, at, :] + tail_decay * (
                dot_nn(key, back_high) + dot_nn(key, back_low)
            )
    dq[...] = grads[0].astype(BF16)
    dk[...] = grads[1].astype(BF16)
    dv[...] = grads[2].astype(BF16)

    for step in range(3, reach + 1):
        pass_on(step)
    for step in range(1, reach + 1):

        @pl.when(me - step >= 0)
        def _():
            for which in range(2):
                pair_copy(which, step).wait()

        @pl.when(me + step < count)
        def _():
            for which in range(2):
                kv_copy(which, step).wait_send()

    for step in (1, 2, 3):

        @pl.when(me + step < count)
        def _():
            state_copy(0, step).wait_send()

        @pl.when(me - step >= 0)
        def _():
            state_copy(1, step).wait_send()

    @pl.when(me + 3 < count)
    def _():
        echo_copy(0).wait_send()

    @pl.when(me - 3 >= 0)
    def _():
        echo_copy(1).wait_send()

    own[0].wait()
    own[1].wait()


def attention_kernel(
    nblocks, reach, heads, chunk, spot,
    q, dout, keys_in, values, dq, dkey, dvalue, scores, probs_grad, flipped,
):
    index = pl.program_id(0)
    width = q.shape[1]
    scale = width ** (-0.5)
    log2e = math.log2(math.e)
    factor = scale * log2e
    total_blocks = keys_in.shape[0] // TILE

    @pl.when(index == 0)
    def _():
        dkey[...] = jnp.zeros(dkey.shape, F32)
        dvalue[...] = jnp.zeros(dvalue.shape, F32)

        @pl.loop(0, total_blocks)
        def _(j):
            at = pl.ds(pl.multiple_of(j * TILE, TILE), TILE)
            flipped[j] = keys_in[at, :].astype(F32).T.astype(BF16)

    per_block = TILE * heads // chunk
    block = index // per_block
    diag = reach * nblocks + block
    first = diag + 1 - spot[block]
    queries = q[...]
    douts = dout[...]

    token = (lax.broadcasted_iota(jnp.int32, (TILE, chunk), 1) + (index % per_block) * chunk) // heads
    seen = lax.broadcasted_iota(jnp.int32, (TILE, chunk), 0) <= token

    def rows_of(j):
        return pl.ds(pl.multiple_of(j * TILE, TILE), TILE)

    def folded(x, op):
        return op(x.reshape(TILE // 8, 8, chunk), axis=0)

    s = jnp.where(seen, dot_nt(keys_in[rows_of(diag), :], queries), NEG)
    scores[diag] = s

    def find_max(j, top):
        s = dot_nt(keys_in[rows_of(j), :], queries)
        scores[j] = s
        return jnp.maximum(top, folded(s, jnp.max))

    top = lax.fori_loop(first, diag, find_max, folded(s, jnp.max))
    top = jnp.max(top, axis=0, keepdims=True) * factor

    def sums(j, carried):
        amount, weighted = carried
        p = jnp.exp2(scores[j] * factor - top)
        g = dot_nt(values[rows_of(j), :], douts)
        scores[j] = p
        probs_grad[j] = g
        return amount + folded(p, jnp.sum), weighted + folded(p * g, jnp.sum)

    zero = jnp.zeros((8, chunk), F32)
    amount, weighted = lax.fori_loop(first, diag + 1, sums, (zero, zero))
    inverse = 1.0 / jnp.sum(amount, axis=0, keepdims=True)
    delta = jnp.sum(weighted, axis=0, keepdims=True) * inverse

    def grads(j, acc):
        p = scores[j] * inverse
        g = p * (probs_grad[j] - delta)
        p = p.astype(BF16)
        g = g.astype(BF16)
        at = rows_of(j)
        dvalue[at, :] += dot_nn(p, douts)
        dkey[at, :] += dot_nn(g, queries)
        return acc + dot_nn(flipped[j], g)

    acc = lax.fori_loop(first, diag + 1, grads, jnp.zeros((width, chunk), F32))
    dq[...] = (acc.T * scale).astype(BF16)


def reduce_kernel(
    count, reach, length, dkey, dvalue, dk, dv, paired, out, inbox,
    pair_send, pair_recv, send_sem, recv_sem,
):
    me = lax.axis_index("ctx")
    core = lax.axis_index("head")
    half = length // 2
    scale = dkey.shape[1] ** (-0.5)
    greet(me, core, count, reach)
    sources = (dkey, dvalue)

    def pair_copy(which, step):
        place = pl.multiple_of((reach - step) * length + (1 - core) * half, half)
        return pltpu.make_async_remote_copy(
            src_ref=sources[which].at[pl.ds(place, half)],
            dst_ref=paired.at[which, step],
            send_sem=pair_send.at[which, step],
            recv_sem=pair_recv.at[which, step],
            device_id={"head": 1 - core},
            device_id_type=MESH,
        )

    def home_copy(step):
        return pltpu.make_async_remote_copy(
            src_ref=out.at[step - 1],
            dst_ref=inbox.at[step - 1],
            send_sem=send_sem.at[step - 1],
            recv_sem=recv_sem.at[step - 1],
            device_id={"ctx": me - step},
            device_id_type=MESH,
        )

    order = list(range(reach, -1, -1))
    for step in order:
        pair_copy(0, step).start()
        pair_copy(1, step).start()

    def mine(which, step):
        place = pl.multiple_of((reach - step) * length + core * half, half)
        return sources[which][pl.ds(place, half), :] + paired[which, step]

    for step in order:
        for which in range(2):
            pair_copy(which, step).wait_recv()
        if step > 0:
            for which in range(2):
                out[step - 1, which] = mine(which, step).astype(BF16)

            @pl.when(me - step >= 0)
            def _():
                home_copy(step).start()

        if step > 0:

            @pl.when(me + step >= count)
            def _():
                inbox[step - 1] = jnp.zeros(inbox.shape[1:], BF16)

    paired[0, 0] = mine(0, 0)
    paired[1, 0] = mine(1, 0)
    for step in range(1, reach + 1):

        @pl.when(me + step < count)
        def _():
            home_copy(step).wait_recv()

        for which in range(2):
            paired[which, 0] += inbox[step - 1, which].astype(F32)
    dk[...] = (paired[0, 0] * scale).astype(BF16)
    dv[...] = paired[1, 0].astype(BF16)
    for step in order:
        pair_copy(0, step).wait_send()
        pair_copy(1, step).wait_send()
        if step > 0:

            @pl.when(me - step >= 0)
            def _():
                home_copy(step).wait_send()


def shards(count, lin_q, lin_k, lin_v, lin_dout, lin_decay, att_q, att_k, att_v, att_dout, doc_block):
    length, heads, width = lin_q.shape
    nblocks = length // TILE
    reach = -(-(MOST - 1) // nblocks)
    half = length // 2
    flat = lambda x: x.reshape(length * heads, width)
    shape = jax.ShapeDtypeStruct
    vmem = pl.BlockSpec(memory_space=pltpu.VMEM)
    smem = pl.BlockSpec(memory_space=pltpu.SMEM)
    anywhere = pl.BlockSpec(memory_space=pl.ANY)
    rows = length * heads
    window = (reach + 1) * length
    state = (heads, width, width)
    packet = (heads, width + 8, width)
    dma = pltpu.SemaphoreType.DMA
    lin_dq, lin_dk, lin_dv, kall, vall = pl.pallas_call(
        functools.partial(lightning_kernel, count, reach, heads, nblocks),
        out_shape=[shape((rows, width), BF16)] * 3 + [shape((window, width), BF16)] * 2,
        in_specs=[smem] + [vmem] * 5 + [anywhere] * 2,
        out_specs=[vmem] * 3 + [anywhere] * 2,
        scratch_shapes=[
            pltpu.VMEM((4, TILE * heads, width), F32),
            pltpu.VMEM((4, nblocks, heads, TILE, width), BF16),
            pltpu.VMEM((3, rows, width), F32),
            pltpu.VMEM((2, nblocks) + state, F32),
            pltpu.VMEM(packet, F32),
            pltpu.VMEM((3,) + packet, F32),
            pltpu.VMEM(packet, F32),
            pltpu.VMEM((3,) + packet, F32),
            pltpu.VMEM(state, F32),
            pltpu.VMEM(state, F32),
            pltpu.VMEM(state, F32),
            pltpu.VMEM(state, F32),
            dma((2,)),
            dma((2, reach)),
            dma((2, reach)),
            dma((2, reach)),
            dma((2, reach)),
            dma((2, 4)),
            dma((2, 4)),
        ],
        compiler_params=pltpu.CompilerParams(
            collective_id=0, has_side_effects=True, vmem_limit_bytes=40 * 1024 * 1024
        ),
        name="lightning",
    )(doc_block, flat(lin_q), flat(lin_k), flat(lin_v), flat(lin_dout), lin_decay, att_k, att_v)

    me = lax.axis_index("ctx")
    here = lax.dynamic_slice_in_dim(doc_block, me * nblocks, nblocks)
    at = me * nblocks + jnp.arange(nblocks, dtype=jnp.int32)
    before = jnp.sum((doc_block[None, :] < here[:, None]).astype(jnp.int32), axis=1)
    spot = at - before + 1
    chunk = 512
    att_dq, dkey, dvalue = pl.pallas_call(
        functools.partial(attention_kernel, nblocks, reach, heads, chunk),
        grid_spec=pltpu.PrefetchScalarGridSpec(
            num_scalar_prefetch=1,
            grid=(rows // chunk,),
            in_specs=[
                pl.BlockSpec((chunk, width), lambda i, s: (i, 0)),
                pl.BlockSpec((chunk, width), lambda i, s: (i, 0)),
                pl.BlockSpec((window, width), lambda i, s: (0, 0)),
                pl.BlockSpec((window, width), lambda i, s: (0, 0)),
            ],
            out_specs=[
                pl.BlockSpec((chunk, width), lambda i, s: (i, 0)),
                pl.BlockSpec((window, width), lambda i, s: (0, 0)),
                pl.BlockSpec((window, width), lambda i, s: (0, 0)),
            ],
            scratch_shapes=[
                pltpu.VMEM((window // TILE, TILE, chunk), F32),
                pltpu.VMEM((window // TILE, TILE, chunk), F32),
                pltpu.VMEM((window // TILE, width, TILE), BF16),
            ],
        ),
        out_shape=[
            shape((rows, width), BF16),
            shape((window, width), F32),
            shape((window, width), F32),
        ],
        compiler_params=pltpu.CompilerParams(vmem_limit_bytes=50 * 1024 * 1024),
        name="attention",
    )(spot, flat(att_q), flat(att_dout), kall, vall)

    att_dk, att_dv = pl.pallas_call(
        functools.partial(reduce_kernel, count, reach, length),
        out_shape=[shape((half, width), BF16)] * 2,
        in_specs=[vmem] * 2,
        out_specs=[vmem] * 2,
        scratch_shapes=[
            pltpu.VMEM((2, reach + 1, half, width), F32),
            pltpu.VMEM((reach, 2, half, width), BF16),
            pltpu.VMEM((reach, 2, half, width), BF16),
            dma((2, reach + 1)),
            dma((2, reach + 1)),
            dma((reach,)),
            dma((reach,)),
        ],
        compiler_params=pltpu.CompilerParams(
            collective_id=1, has_side_effects=True, vmem_limit_bytes=40 * 1024 * 1024
        ),
        name="reduce",
    )(dkey, dvalue)
    full = lambda x: x.reshape(length, heads, width)
    return (full(lin_dq), full(lin_dk), full(lin_dv), full(att_dq), att_dk, att_dv)


def solution(mesh):
    return jax.shard_map(
        functools.partial(shards, mesh.shape["ctx"]),
        mesh=mesh,
        in_specs=(
            P("ctx", "head", None),
            P("ctx", "head", None),
            P("ctx", "head", None),
            P("ctx", "head", None),
            P("head", "ctx"),
            P("ctx", "head", None),
            P("ctx", None),
            P("ctx", None),
            P("ctx", "head", None),
            P(),
        ),
        out_specs=(
            P("ctx", "head", None),
            P("ctx", "head", None),
            P("ctx", "head", None),
            P("ctx", "head", None),
            P(("ctx", "head"), None),
            P(("ctx", "head"), None),
        ),
        check_vma=False,
    )
```

time: 371 us -> 138 us (0.37)
  starting transfers between devices: 131 us -> 0 us
  Pallas kernels: 0 us -> 121 us
  waiting for transfers between devices: 89.4 us -> 0 us
  matrix products: 71.5 us -> 0 us
  other arithmetic: 33.1 us -> 0.84 us
  between operations: 15.7 us -> 0.69 us
  local copies, waits for them, and re-layouts: 26.1 us -> 14.7 us
    ppermute x43 -> x0, starting transfers between devices: 131 us -> none  [the longest x36 125 us: shifted(): lax.ppermute(value, axis, [(source, source + steps) for source in range(f...]
    pallas_call x0 -> x3, Pallas kernels: none -> 121 us  [the longest x1 57.1 us: shards(): pl.pallas_call(functools.partial(lightning_kernel, count, reach, heads, n...]
    ppermute x43 -> x0, waiting for transfers between devices: 82 us -> none  [the longest x36 56.5 us: shifted(): lax.ppermute(value, axis, [(source, source + steps) for source in range(f...]
    dot_general x56 -> x0, matrix products: 71.5 us -> none  [the longest x7 14.4 us: gather_stats(): jnp.einsum('thd,sd->hts', att_dout, values, preferred_element_type=jnp.fl...]
    add x47 -> x1, other arithmetic: 7.97 us -> 0.01 us  [shards(): spot = at - before + 1]
    reduce_scatter x1 -> x0, waiting for transfers between devices: 7.41 us -> none  [attention(): travel = lax.psum_scatter(travel, 'head', scatter_dimension=1, tiled=True)]
    another operation x7 -> x0, other arithmetic: 7.04 us -> none
    convert_element_type x4 -> x0, other arithmetic: 6.72 us -> none  [the longest x1 3.49 us: grad_terms(): grad_b = grad_scores.astype(jnp.bfloat16)]
  transfers between devices with their start and end apart: 44 -> 0, of which waited for: 30 -> 0; matrix products, arithmetic and copies ran while one was open for 24% -> 0% of each run, Pallas kernels for 0% -> 0%
where the time goes in v1:
time: 138 us; the launch traced here: 137 us
  Pallas kernels  121 us (88%)
  local copies, waits for them, and re-layouts  14.7 us (11%)
    pallas_call x1, Pallas kernels, shards(): pl.pallas_call(functools.partial(lightning_kernel, count, reach, heads, n...  57.1 us
    pallas_call x1, Pallas kernels, shards(): pl.pallas_call(functools.partial(reduce_kernel, count, reach, length), ou...  34.3 us
    pallas_call x1, Pallas kernels, shards(): pl.pallas_call(functools.partial(attention_kernel, nblocks, reach, heads,...  29.5 us
    unnamed x29, local copies, waits for them, and re-layouts  14 us

profile of v1, /device:TPU:7, one launch (start us, length us, event | category | flops | bytes accessed | tf_op | source)
XLA Modules:
  0.0 137.2 jit_solution(8734602246342080159)
XLA Ops:
  0.6 0.7 dynamic_slice.3
  1.4 0.8 fusion
  2.2 0.0 copy-start.2
  2.2 1.0 copy-done.2
  3.3 0.0 copy-start.3
  3.3 1.0 copy-done.3
  4.3 0.0 copy-start.4
  4.3 1.0 copy-done.4
  5.3 0.0 copy-start.5
  5.3 1.0 copy-done.5
  6.4 0.0 copy-start.8
  6.4 0.9 copy-done.8
  7.3 0.0 copy-start.9
  7.3 0.9 copy-done.9
  8.2 0.0 copy-start.10
  8.2 0.7 copy-done.10
  8.9 0.0 copy-start.11
  8.9 0.7 copy-done.11
  9.5 0.0 copy-start.6
  9.5 0.0 copy-start.7
  9.6 57.1 %lightning.1 = (bf16[2048,128]{1,0:T(8,128)(2,1)S(1)}, bf16[2048,128]{1,0:T(8,128)(2,1)S(1)}, bf16[2048,128]{1,0:T(8,128)(2,1)S(1)}, bf16[3584,128]{1,0:T(8,128)(2,1)S(1)}, bf16[3584,128]{1,0:T(8,128)(2,1)S(1)}) custom-call(s32[32]{0:T(128)S(1)} %copy-done.11, bf16[2048,128]{1,0:T(8,128)(2,1)S(1)} %bitcast.13, bf16[2048,128]{1,0:T(8,128)(2,1)S(1)} %bitcast.14, ...), custom_call_target="tpu_custom_call" | custom-call | tf_op jit(solution)/shard_map/lightning/pallas_call | solution.py:532
  66.7 0.0 copy-done.6
  66.7 0.0 copy-done.7
  66.7 29.5 %attention.1 = (bf16[2048,128]{1,0:T(8,128)(2,1)}, f32[3584,128]{1,0:T(8,128)}, f32[3584,128]{1,0:T(8,128)}) custom-call(s32[2]{0:T(128)S(1)} %subtract_add_fusion.spot, bf16[2048,128]{1,0:T(8,128)(2,1)S(1)} %bitcast.17, bf16[2048,128]{1,0:T(8,128)(2,1)S(1)} %bitcast.18, bf16[3584,128]{1,0:T(8,128)(2,1)S(1)} %get-tuple-element.19.keys_in, ...), custom_call_target="tpu_custom_call" | custom-call | tf_op jit(solution)/shard_map/attention/pallas_call | solution.py:570
  96.2 0.0 copy-start
  96.3 1.5 %copy-done = f32[3584,128]{1,0:T(8,128)S(1)} copy-done((f32[3584,128]{1,0:T(8,128)S(1)}, f32[3584,128]{1,0:T(8,128)}, u32[]{:S(2)}) %copy-start) | copy-done | bytes 1835032
  97.7 0.0 copy-start.1
  97.8 1.5 %copy-done.1 = f32[3584,128]{1,0:T(8,128)S(1)} copy-done((f32[3584,128]{1,0:T(8,128)S(1)}, f32[3584,128]{1,0:T(8,128)}, u32[]{:S(2)}) %copy-start.1) | copy-done | bytes 1835032
  99.2 34.3 %reduce.1 = (bf16[256,128]{1,0:T(8,128)(2,1)S(1)}, bf16[256,128]{1,0:T(8,128)(2,1)S(1)}) custom-call(f32[3584,128]{1,0:T(8,128)S(1)} %copy-done, f32[3584,128]{1,0:T(8,128)S(1)} %copy-done.1), custom_call_target="tpu_custom_call" | custom-call | tf_op jit(solution)/shard_map/reduce/pallas_call | solution.py:601
  133.6 0.8 copy.21
  134.4 0.8 copy.22
  135.1 0.8 copy.23
  135.9 0.6 copy.24
  136.6 0.6 copy.25
  (1 shorter events, 0.0 us)
Async XLA Ops:
  2.2 1.0 copy-start.2
  3.3 1.0 copy-start.3
  4.3 1.0 copy-start.4
  5.3 1.0 copy-start.5
  6.4 0.9 copy-start.8
  7.3 0.9 copy-start.9
  8.2 0.7 copy-start.10
  8.9 0.7 copy-start.11
  9.5 57.1 %copy-start.6 = (bf16[512,4,128]{2,1,0:T(4,128)(2,1)S(1)}, bf16[512,4,128]{2,1,0:T(4,128)(2,1)}, u32[]{:S(2)}) copy-start(bf16[512,4,128]{2,1,0:T(4,128)(2,1)} %param.15) | copy-start | bytes 1572868
  9.5 57.1 %copy-start.7 = (bf16[512,4,128]{2,1,0:T(4,128)(2,1)S(1)}, bf16[512,4,128]{2,1,0:T(4,128)(2,1)}, u32[]{:S(2)}) copy-start(bf16[512,4,128]{2,1,0:T(4,128)(2,1)} %param.18) | copy-start | bytes 1572868
  96.2 1.5 %copy-start = (f32[3584,128]{1,0:T(8,128)S(1)}, f32[3584,128]{1,0:T(8,128)}, u32[]{:S(2)}) copy-start(f32[3584,128]{1,0:T(8,128)} %get-tuple-element.22.dkey) | copy-start | bytes 5505028
  97.7 1.5 %copy-start.1 = (f32[3584,128]{1,0:T(8,128)S(1)}, f32[3584,128]{1,0:T(8,128)}, u32[]{:S(2)}) copy-start(f32[3584,128]{1,0:T(8,128)} %get-tuple-element.23.dvalue) | copy-start | bytes 5505028

commit v2 on v1

v2 whole, which is shorter than its diff:
```python
import functools
import math

import jax
import jax.numpy as jnp
from jax import lax
from jax.experimental import pallas as pl
from jax.experimental.pallas import tpu as pltpu
from jax.sharding import PartitionSpec as P

TILE = 256
MOST = 12
NEG = -1e30
MESH = pl.DeviceIdType.MESH
F32 = jnp.float32
BF16 = jnp.bfloat16
SHAPE = jax.ShapeDtypeStruct
DMA = pltpu.SemaphoreType.DMA
IN_VMEM = pl.BlockSpec(memory_space=pltpu.VMEM)
IN_SMEM = pl.BlockSpec(memory_space=pltpu.SMEM)
ANYWHERE = pl.BlockSpec(memory_space=pl.ANY)
VMEM_LIMIT = 56 * 1024 * 1024


def dot_nn(a, b):
    return lax.dot_general(a, b, (((1,), (0,)), ((), ())), preferred_element_type=F32)


def dot_nt(a, b):
    return lax.dot_general(a, b, (((1,), (1,)), ((), ())), preferred_element_type=F32)


def dot_tn(a, b):
    return lax.dot_general(a, b, (((0,), (0,)), ((), ())), preferred_element_type=F32)


def split(x):
    high = x.astype(BF16)
    return high, (x - high.astype(F32)).astype(BF16)


def greet(me, core, count, reach):
    barrier = pltpu.get_barrier_semaphore()
    pl.semaphore_signal(barrier, inc=1, device_id={"head": 1 - core}, device_id_type=MESH)
    for step in range(1, reach + 1):

        @pl.when(me + step < count)
        def _():
            pl.semaphore_signal(barrier, inc=1, device_id={"ctx": me + step}, device_id_type=MESH)

        @pl.when(me - step >= 0)
        def _():
            pl.semaphore_signal(barrier, inc=1, device_id={"ctx": me - step}, device_id_type=MESH)

    pl.semaphore_wait(
        barrier, 1 + jnp.minimum(me, reach) + jnp.minimum(count - 1 - me, reach)
    )


def decay_terms(me, count, nblocks, doc, dec):
    t_sub = lax.broadcasted_iota(jnp.int32, (TILE, TILE), 0)
    t_lane = lax.broadcasted_iota(jnp.int32, (TILE, TILE), 1)
    upper = (t_sub <= t_lane).astype(F32)
    lower = (t_sub >= t_lane).astype(F32)

    def link(at_one, at_two):
        one = jnp.clip(at_one, 0, count * nblocks - 1)
        two = jnp.clip(at_two, 0, count * nblocks - 1)
        inside = jnp.logical_and(at_one >= 0, at_two < count * nblocks)
        same = jnp.logical_and(doc[one] == doc[two], inside)
        return jnp.where(same, 1.0, 0.0).astype(F32)

    follows = [link(me * nblocks + b - 1, me * nblocks + b) for b in range(nblocks)]
    precedes = [link(me * nblocks + b, me * nblocks + b + 1) for b in range(nblocks)]

    cum_row, cum_col = [], []
    for b in range(nblocks):
        piece = dec[:, b * TILE : (b + 1) * TILE]
        cum_row.append(
            lax.dot_general(
                piece, upper, (((1,), (0,)), ((), ())),
                preferred_element_type=F32, precision=lax.Precision.HIGHEST,
            )
        )
        cum_col.append(
            lax.dot_general(
                lower, piece, (((1,), (1,)), ((), ())),
                preferred_element_type=F32, precision=lax.Precision.HIGHEST,
            )
        )

    def head_terms(b, h):
        row = cum_row[b][h : h + 1, :]
        col = cum_col[b][:, h : h + 1]
        total = col[TILE - 1 : TILE, :]
        return row, col, total

    return follows, precedes, head_terms, t_sub, t_lane


def lightning_kernel(
    count, reach, heads, nblocks,
    doc, lq, lk, lv, ld, dec_in, att_k, att_v,
    send_l, send_r, parts, states, kall, vall,
    wide, raw, dec, raw_sem, own_sem, kv_send, kv_recv, pair_send, pair_recv,
):
    me = lax.axis_index("ctx")
    core = lax.axis_index("head")
    length = nblocks * TILE
    half = length // 2
    width = lq.shape[1]
    rows = TILE * heads
    loads = [
        pltpu.make_async_copy(ref, raw.at[a], raw_sem.at[a])
        for a, ref in enumerate((lq, lk, lv, ld))
    ]
    loads.append(pltpu.make_async_copy(dec_in, dec, raw_sem.at[4]))
    for load in loads:
        load.start()
    greet(me, core, count, reach)

    pairs = ((att_k, kall), (att_v, vall))
    start = pl.multiple_of(core * half, half)

    def kv_copy(which, step):
        source, target = pairs[which]
        place = pl.multiple_of((reach - step) * length + core * half, half)
        return pltpu.make_async_remote_copy(
            src_ref=source.at[pl.ds(start, half)],
            dst_ref=target.at[pl.ds(place, half)],
            send_sem=kv_send.at[which, step - 1],
            recv_sem=kv_recv.at[which, step - 1],
            device_id={"ctx": me + step},
            device_id_type=MESH,
        )

    def pair_copy(which, step):
        target = pairs[which][1]
        place = pl.multiple_of((reach - step) * length + core * half, half)
        return pltpu.make_async_remote_copy(
            src_ref=target.at[pl.ds(place, half)],
            dst_ref=target.at[pl.ds(place, half)],
            send_sem=pair_send.at[which, step - 1],
            recv_sem=pair_recv.at[which, step - 1],
            device_id={"head": 1 - core},
            device_id_type=MESH,
        )

    for step in range(1, reach + 1):

        @pl.when(me + step < count)
        def _():
            kv_copy(0, step).start()
            kv_copy(1, step).start()

    own = [
        pltpu.make_async_copy(
            pairs[which][0], pairs[which][1].at[pl.ds(reach * length, length)], own_sem.at[which]
        )
        for which in range(2)
    ]
    own[0].start()
    own[1].start()

    for load in loads:
        load.wait()
    follows, precedes, head_terms, _, _ = decay_terms(me, count, nblocks, doc, dec)

    for b in range(nblocks):
        for a in range(4):
            wide[a] = raw[a, b * rows : (b + 1) * rows, :].astype(F32)
        for h in range(heads):
            row, col, total = head_terms(b, h)
            picked = [wide[a, pl.ds(h, TILE, stride=heads), :] for a in range(4)]
            for a in range(4):
                parts[a, b, h] = picked[a].astype(BF16)
            key_high, key_low = split((picked[1] * jnp.exp(total - col)).T)
            value = picked[2].astype(BF16)
            states[0, b, h] = dot_nn(key_high, value) + dot_nn(key_low, value)
            query_high, query_low = split((picked[0] * jnp.exp(col)).T)
            dout = picked[3].astype(BF16)
            states[1, b, h] = dot_nn(query_high, dout) + dot_nn(query_low, dout)

    for h in range(heads):
        keep = [jnp.exp(head_terms(b, h)[2]) for b in range(nblocks)]
        total_l = states[0, 0, h]
        mult_l = keep[0] * follows[0]
        for b in range(1, nblocks):
            total_l = states[0, b, h] + keep[b] * follows[b] * total_l
            mult_l = mult_l * keep[b] * follows[b]
        total_r = states[1, nblocks - 1, h]
        mult_r = keep[nblocks - 1] * precedes[nblocks - 1]
        for b in reversed(range(nblocks - 1)):
            total_r = states[1, b, h] + keep[b] * precedes[b] * total_r
            mult_r = mult_r * keep[b] * precedes[b]
        for send, total, mult in ((send_l, total_l, mult_l), (send_r, total_r, mult_r)):
            high, low = split(jnp.broadcast_to(mult, (16, width)))
            send[h, 0:width, :] = total.astype(BF16)
            send[h, width : width + 16, :] = high
            send[h, width + 16 : width + 32, :] = low

    def pass_on(step):
        @pl.when(me - step >= 0)
        def _():
            for which in range(2):
                kv_copy(which, step).wait_recv()
                pair_copy(which, step).start()

    for step in range(1, reach + 1):
        pass_on(step)
    for step in range(1, reach + 1):

        @pl.when(me - step >= 0)
        def _():
            for which in range(2):
                pair_copy(which, step).wait()

        @pl.when(me + step < count)
        def _():
            for which in range(2):
                kv_copy(which, step).wait_send()

    own[0].wait()
    own[1].wait()


def attention_kernel(
    nblocks, reach, heads, chunk, spot,
    q, dout, keys_in, values, dq, dkey, dvalue, scores, probs_grad, flipped,
):
    index = pl.program_id(0)
    width = q.shape[1]
    scale = width ** (-0.5)
    log2e = math.log2(math.e)
    factor = scale * log2e
    total_blocks = keys_in.shape[0] // TILE

    @pl.when(index == 0)
    def _():
        dkey[...] = jnp.zeros(dkey.shape, F32)
        dvalue[...] = jnp.zeros(dvalue.shape, F32)

        @pl.loop(0, total_blocks)
        def _(j):
            at = pl.ds(pl.multiple_of(j * TILE, TILE), TILE)
            flipped[j] = keys_in[at, :].astype(F32).T.astype(BF16)

    per_block = TILE * heads // chunk
    block = index // per_block
    diag = reach * nblocks + block
    first = diag + 1 - spot[block]
    queries = q[...]
    douts = dout[...]

    token = (lax.broadcasted_iota(jnp.int32, (TILE, chunk), 1) + (index % per_block) * chunk) // heads
    seen = lax.broadcasted_iota(jnp.int32, (TILE, chunk), 0) <= token

    def rows_of(j):
        return pl.ds(pl.multiple_of(j * TILE, TILE), TILE)

    def folded(x, op):
        return op(x.reshape(TILE // 8, 8, chunk), axis=0)

    s = jnp.where(seen, dot_nt(keys_in[rows_of(diag), :], queries), NEG)
    scores[diag] = s

    def find_max(j, top):
        s = dot_nt(keys_in[rows_of(j), :], queries)
        scores[j] = s
        return jnp.maximum(top, folded(s, jnp.max))

    top = lax.fori_loop(first, diag, find_max, folded(s, jnp.max))
    top = jnp.max(top, axis=0, keepdims=True) * factor

    def sums(j, carried):
        amount, weighted = carried
        p = jnp.exp2(scores[j] * factor - top)
        g = dot_nt(values[rows_of(j), :], douts)
        scores[j] = p
        probs_grad[j] = g
        return amount + folded(p, jnp.sum), weighted + folded(p * g, jnp.sum)

    zero = jnp.zeros((8, chunk), F32)
    amount, weighted = lax.fori_loop(first, diag + 1, sums, (zero, zero))
    inverse = 1.0 / jnp.sum(amount, axis=0, keepdims=True)
    delta = jnp.sum(weighted, axis=0, keepdims=True) * inverse

    def grads(j, acc):
        p = scores[j] * inverse
        g = p * (probs_grad[j] - delta)
        p = p.astype(BF16)
        g = g.astype(BF16)
        at = rows_of(j)
        dvalue[at, :] += dot_nn(p, douts)
        dkey[at, :] += dot_nn(g, queries)
        return acc + dot_nn(flipped[j], g)

    acc = lax.fori_loop(first, diag + 1, grads, jnp.zeros((width, chunk), F32))
    dq[...] = (acc.T * scale).astype(BF16)


def reduce_kernel(
    count, reach, heads, nblocks,
    doc, dec, parts, states, got_l1, got_l2, got_l3, got_r1, got_r2, got_r3, dkey, dvalue,
    dq, dk, dv, att_dk, att_dv,
    grads, near, echo, land, paired, out, inbox,
    pair_send, pair_recv, send_sem, recv_sem, echo_send, echo_recv,
):
    me = lax.axis_index("ctx")
    core = lax.axis_index("head")
    length = nblocks * TILE
    half = length // 2
    rows = TILE * heads
    width = dkey.shape[1]
    scale = dkey.shape[1] ** (-0.5)
    greet(me, core, count, reach)
    sources = (dkey, dvalue)

    def pair_copy(which, step):
        place = pl.multiple_of((reach - step) * length + (1 - core) * half, half)
        return pltpu.make_async_remote_copy(
            src_ref=sources[which].at[pl.ds(place, half)],
            dst_ref=paired.at[which, step],
            send_sem=pair_send.at[which, step],
            recv_sem=pair_recv.at[which, step],
            device_id={"head": 1 - core},
            device_id_type=MESH,
        )

    def home_copy(step):
        return pltpu.make_async_remote_copy(
            src_ref=out.at[step - 1],
            dst_ref=inbox.at[step - 1],
            send_sem=send_sem.at[step - 1],
            recv_sem=recv_sem.at[step - 1],
            device_id={"ctx": me - step},
            device_id_type=MESH,
        )

    order = list(range(reach, -1, -1))
    for step in order:
        pair_copy(0, step).start()
        pair_copy(1, step).start()

    follows, precedes, head_terms, t_sub, t_lane = decay_terms(me, count, nblocks, doc, dec)

    def echo_copy(side):
        return pltpu.make_async_remote_copy(
            src_ref=echo.at[side],
            dst_ref=land.at[side],
            send_sem=echo_send.at[side],
            recv_sem=echo_recv.at[side],
            device_id={"ctx": me + 3 if side == 0 else me - 3},
            device_id_type=MESH,
        )

    spans = ([], [])
    for side, got in enumerate(((got_l1, got_l2, got_l3), (got_r1, got_r2, got_r3))):
        for h in range(heads):
            mult = [
                ref[h, width : width + 16, :].astype(F32)[0:1]
                + ref[h, width + 16 : width + 32, :].astype(F32)[0:1]
                for ref in got
            ]
            one, two, three = (ref[h, 0:width, :].astype(F32) for ref in got)
            total = one + mult[0] * (two + mult[1] * three)
            near[side, h] = total
            echo[side, h] = total.astype(BF16)
            spans[side].append(mult[0] * mult[1] * mult[2])

    before = (me - 3 >= 0, me + 3 < count)
    after = (me + 3 < count, me - 3 >= 0)
    for side in range(2):

        @pl.when(after[side])
        def _():
            echo_copy(side).start()

        @pl.when(jnp.logical_not(before[side]))
        def _():
            land[side] = jnp.zeros(land.shape[1:], BF16)

    def within(b):
        for h in range(heads):
            row, col, total = head_terms(b, h)
            query, key, value, dout = (parts[a, b, h] for a in range(4))
            seen = t_sub <= t_lane
            weight = jnp.where(seen, jnp.exp(jnp.where(seen, row - col, 0.0)), 0.0)
            left = (dot_nt(value, dout) * weight).astype(BF16)
            right = (dot_nt(key, query) * weight).astype(BF16)
            at = pl.ds(b * rows + h, TILE, stride=heads)
            grads[0, at, :] = dot_tn(left, key)
            grads[1, at, :] = dot_nn(left, query)
            grads[2, at, :] = dot_nn(right, dout)

    within(0)

    def mine(which, step):
        place = pl.multiple_of((reach - step) * length + core * half, half)
        return sources[which][pl.ds(place, half), :] + paired[which, step]

    for step in order:
        for which in range(2):
            pair_copy(which, step).wait_recv()
        if step > 0:
            for which in range(2):
                out[step - 1, which] = mine(which, step).astype(BF16)

            @pl.when(me - step >= 0)
            def _():
                home_copy(step).start()

        if step > 0:

            @pl.when(me + step >= count)
            def _():
                inbox[step - 1] = jnp.zeros(inbox.shape[1:], BF16)

    for b in range(1, nblocks):
        within(b)
    for side in range(2):

        @pl.when(before[side])
        def _():
            echo_copy(side).wait_recv()

    for h in range(heads):
        keep = [jnp.exp(head_terms(b, h)[2]) for b in range(nblocks)]
        state = near[0, h] + spans[0][h] * land[0, h].astype(F32)
        into = []
        for b in range(nblocks):
            into.append(follows[b] * state)
            state = states[0, b, h] + keep[b] * into[b]
        state = near[1, h] + spans[1][h] * land[1, h].astype(F32)
        back = [None] * nblocks
        for b in reversed(range(nblocks)):
            back[b] = precedes[b] * state
            state = states[1, b, h] + keep[b] * back[b]
        for b in range(nblocks):
            row, col, total = head_terms(b, h)
            query, key, value, dout = (parts[a, b, h] for a in range(4))
            head_decay = jnp.exp(col)
            tail_decay = jnp.exp(total - col)
            into_high, into_low = split(into[b])
            back_high, back_low = split(back[b])
            at = pl.ds(b * rows + h, TILE, stride=heads)
            grads[0, at, :] = grads[0, at, :] + head_decay * (
                dot_nt(dout, into_high) + dot_nt(dout, into_low)
            )
            grads[1, at, :] = grads[1, at, :] + tail_decay * (
                dot_nt(value, back_high) + dot_nt(value, back_low)
            )
            grads[2, at, :] = grads[2, at, :] + tail_decay * (
                dot_nn(key, back_high) + dot_nn(key, back_low)
            )
    dq[...] = grads[0].astype(BF16)
    dk[...] = grads[1].astype(BF16)
    dv[...] = grads[2].astype(BF16)

    paired[0, 0] = mine(0, 0)
    paired[1, 0] = mine(1, 0)
    for step in range(1, reach + 1):

        @pl.when(me + step < count)
        def _():
            home_copy(step).wait_recv()

        for which in range(2):
            paired[which, 0] += inbox[step - 1, which].astype(F32)
    att_dk[...] = (paired[0, 0] * scale).astype(BF16)
    att_dv[...] = paired[1, 0].astype(BF16)
    for step in order:
        pair_copy(0, step).wait_send()
        pair_copy(1, step).wait_send()
        if step > 0:

            @pl.when(me - step >= 0)
            def _():
                home_copy(step).wait_send()
    for side in range(2):

        @pl.when(after[side])
        def _():
            echo_copy(side).wait_send()


def call_lightning(count, lin_q, lin_k, lin_v, lin_dout, lin_decay, att_k, att_v, doc_block):
    length, heads, width = lin_q.shape
    nblocks = length // TILE
    reach = -(-(MOST - 1) // nblocks)
    rows = length * heads
    window = (reach + 1) * length
    state = (heads, width, width)
    flat = lambda x: x.reshape(rows, width)
    return pl.pallas_call(
        functools.partial(lightning_kernel, count, reach, heads, nblocks),
        out_shape=[
            SHAPE((heads, width + 32, width), BF16),
            SHAPE((heads, width + 32, width), BF16),
            SHAPE((4, nblocks, heads, TILE, width), BF16),
            SHAPE((2, nblocks) + state, F32),
            SHAPE((window, width), BF16),
            SHAPE((window, width), BF16),
        ],
        in_specs=[IN_SMEM] + [ANYWHERE] * 7,
        out_specs=[IN_VMEM] * 4 + [ANYWHERE] * 2,
        scratch_shapes=[
            pltpu.VMEM((4, TILE * heads, width), F32),
            pltpu.VMEM((4, rows, width), BF16),
            pltpu.VMEM(lin_decay.shape, F32),
            DMA((5,)),
            DMA((2,)),
            DMA((2, reach)),
            DMA((2, reach)),
            DMA((2, reach)),
            DMA((2, reach)),
        ],
        compiler_params=pltpu.CompilerParams(
            collective_id=0, has_side_effects=True, vmem_limit_bytes=VMEM_LIMIT
        ),
        name="lightning",
    )(doc_block, flat(lin_q), flat(lin_k), flat(lin_v), flat(lin_dout), lin_decay, att_k, att_v)


def call_attention(chunk, spot, att_q, att_dout, kall, vall):
    length, heads, width = att_q.shape
    nblocks = length // TILE
    rows = length * heads
    window = kall.shape[0]
    reach = window // length - 1
    flat = lambda x: x.reshape(rows, width)
    return pl.pallas_call(
        functools.partial(attention_kernel, nblocks, reach, heads, chunk),
        grid_spec=pltpu.PrefetchScalarGridSpec(
            num_scalar_prefetch=1,
            grid=(rows // chunk,),
            in_specs=[
                pl.BlockSpec((chunk, width), lambda i, s: (i, 0)),
                pl.BlockSpec((chunk, width), lambda i, s: (i, 0)),
                pl.BlockSpec((window, width), lambda i, s: (0, 0)),
                pl.BlockSpec((window, width), lambda i, s: (0, 0)),
            ],
            out_specs=[
                pl.BlockSpec((chunk, width), lambda i, s: (i, 0)),
                pl.BlockSpec((window, width), lambda i, s: (0, 0)),
                pl.BlockSpec((window, width), lambda i, s: (0, 0)),
            ],
            scratch_shapes=[
                pltpu.VMEM((window // TILE, TILE, chunk), F32),
                pltpu.VMEM((window // TILE, TILE, chunk), F32),
                pltpu.VMEM((window // TILE, width, TILE), BF16),
            ],
        ),
        out_shape=[
            SHAPE((rows, width), BF16),
            SHAPE((window, width), F32),
            SHAPE((window, width), F32),
        ],
        compiler_params=pltpu.CompilerParams(vmem_limit_bytes=50 * 1024 * 1024),
        cost_estimate=pl.CostEstimate(
            flops=10 * width * rows * window, bytes_accessed=8 * window * width, transcendentals=0
        ),
        name="attention",
    )(spot, flat(att_q), flat(att_dout), kall, vall)


def shards(count, lin_q, lin_k, lin_v, lin_dout, lin_decay, att_q, att_k, att_v, att_dout, doc_block):
    length, heads, width = lin_q.shape
    nblocks = length // TILE
    reach = -(-(MOST - 1) // nblocks)
    half = length // 2
    rows = length * heads
    window = (reach + 1) * length
    send_l, send_r, parts, states, kall, vall = call_lightning(
        count, lin_q, lin_k, lin_v, lin_dout, lin_decay, att_k, att_v, doc_block
    )
    got = [
        lax.ppermute(send_l, "ctx", [(i, i + step) for i in range(count - step)])
        for step in (1, 2, 3)
    ] + [
        lax.ppermute(send_r, "ctx", [(i + step, i) for i in range(count - step)])
        for step in (1, 2, 3)
    ]
    me = lax.axis_index("ctx")
    here = lax.dynamic_slice_in_dim(doc_block, me * nblocks, nblocks)
    at = me * nblocks + jnp.arange(nblocks, dtype=jnp.int32)
    before = jnp.sum((doc_block[None, :] < here[:, None]).astype(jnp.int32), axis=1)
    spot = at - before + 1
    att_dq, dkey, dvalue = call_attention(1024, spot, att_q, att_dout, kall, vall)
    lin_dq, lin_dk, lin_dv, att_dk, att_dv = pl.pallas_call(
        functools.partial(reduce_kernel, count, reach, heads, nblocks),
        out_shape=[SHAPE((rows, width), BF16)] * 3 + [SHAPE((half, width), BF16)] * 2,
        in_specs=[IN_SMEM] + [IN_VMEM] * 11,
        out_specs=[IN_VMEM] * 5,
        scratch_shapes=[
            pltpu.VMEM((3, rows, width), F32),
            pltpu.VMEM((2, heads, width, width), F32),
            pltpu.VMEM((2, heads, width, width), BF16),
            pltpu.VMEM((2, heads, width, width), BF16),
            pltpu.VMEM((2, reach + 1, half, width), F32),
            pltpu.VMEM((reach, 2, half, width), BF16),
            pltpu.VMEM((reach, 2, half, width), BF16),
            DMA((2, reach + 1)),
            DMA((2, reach + 1)),
            DMA((reach,)),
            DMA((reach,)),
            DMA((2,)),
            DMA((2,)),
        ],
        compiler_params=pltpu.CompilerParams(
            collective_id=1, has_side_effects=True, vmem_limit_bytes=40 * 1024 * 1024
        ),
        name="reduce",
    )(doc_block, lin_decay, parts, states, *got, dkey, dvalue)
    full = lambda x: x.reshape(length, heads, width)
    return (full(lin_dq), full(lin_dk), full(lin_dv), full(att_dq), att_dk, att_dv)


def solution(mesh):
    return jax.shard_map(
        functools.partial(shards, mesh.shape["ctx"]),
        mesh=mesh,
        in_specs=(
            P("ctx", "head", None),
            P("ctx", "head", None),
            P("ctx", "head", None),
            P("ctx", "head", None),
            P("head", "ctx"),
            P("ctx", "head", None),
            P("ctx", None),
            P("ctx", None),
            P("ctx", "head", None),
            P(),
        ),
        out_specs=(
            P("ctx", "head", None),
            P("ctx", "head", None),
            P("ctx", "head", None),
            P("ctx", "head", None),
            P(("ctx", "head"), None),
            P(("ctx", "head"), None),
        ),
        check_vma=False,
    )
```

time: 138 us -> 117 us (0.85); the launches traced: 137 us -> 115 us
  Pallas kernels: 121 us -> 83.5 us
  starting transfers between devices: 0 us -> 21 us
  local copies, waits for them, and re-layouts: 14.7 us -> 9.08 us
    pallas_call x3, Pallas kernels: 121 us -> 83.5 us  [the longest x1 38.8 us: shards(): pl.pallas_call(functools.partial(reduce_kernel, count, reach, heads, nblo...]
    ppermute x0 -> x6, starting transfers between devices: none -> 21 us  [the longest x3 13.9 us: shards(): lax.ppermute(send_l, 'ctx', [(i, i + step) for i in range(count - step)])]
    unnamed x29 -> x25, local copies, waits for them, and re-layouts: 14 us -> 9 us
  transfers between devices with their start and end apart: 0 -> 6, of which waited for: 0 -> 0; matrix products, arithmetic and copies ran while one was open for 0% -> 0% of each run, Pallas kernels for 0% -> 20%
where the time goes in v2:
time: 117 us; the launch traced here: 115 us
  Pallas kernels  83.5 us (71%)
  starting transfers between devices  21 us (18%)
  local copies, waits for them, and re-layouts  9.08 us (8%)
    pallas_call x1, Pallas kernels, shards(): pl.pallas_call(functools.partial(reduce_kernel, count, reach, heads, nblo...  38.8 us
    pallas_call x1, Pallas kernels, call_attention(): pl.pallas_call(functools.partial(attention_kernel, nblocks, reach, heads,...  22.7 us
    pallas_call x1, Pallas kernels, call_lightning(): pl.pallas_call(functools.partial(lightning_kernel, count, reach, heads, n...  22 us
    ppermute x3, starting transfers between devices, shards(): lax.ppermute(send_l, 'ctx', [(i, i + step) for i in range(count - step)])  13.9 us
    unnamed x25, local copies, waits for them, and re-layouts  9 us
    ppermute x3, starting transfers between devices, shards(): lax.ppermute(send_r, 'ctx', [(i + step, i) for i in range(count - step)])  7.11 us
  transfers between devices with their start and end apart: 6, of which 0 were waited for; matrix products, arithmetic and copies ran while one was open for 0% of the time, Pallas kernels for 20%

profile of v2, /device:TPU:7, one launch (start us, length us, event | category | flops | bytes accessed | tf_op | source)
XLA Modules:
  0.0 114.6 jit_solution(7278445209447544199)
XLA Ops:
  0.6 0.0 copy-start.5
  0.6 0.0 copy-start.8
  0.7 0.0 copy-start.9
  0.7 22.0 %lightning.1 = (bf16[4,160,128]{2,1,0:T(8,128)(2,1)}, bf16[4,160,128]{2,1,0:T(8,128)(2,1)}, bf16[4,2,4,256,128]{4,3,2,1,0:T(8,128)(2,1)}, f32[2,2,4,128,128]{4,3...) custom-call(s32[32]{0:T(128)} %doc.3, bf16[2048,128]{1,0:T(8,128)(2,1)} %bitcast.15, ...), custom_call_target="tpu_custom_call" | custom-call | tf_op jit(solution)/shard_map/lightning/pallas_call | solution.py:495
  22.7 1.9 %collective-permute-start = (bf16[4,160,128]{2,1,0:T(8,128)(2,1)}, bf16[4,160,128]{2,1,0:T(8,128)(2,1)S(1)}, u32[]{:S(2)}, u32[]{:S(2)}) collective-permute-start(bf16[4,160,128]{2,1,0:T(8,128)(2,1)} %get-tuple-element.22), channel_id=1, source_target_pairs={{0,2},{2,4},{4,6},{6,8},{8,10},{10,12},{12,14},{14,16},{16,18},{18... | collective-permute-start | bytes 491528 | tf_op jit(solution)/shard_map/ppermute | solution.py:578
  24.6 4.3 %collective-permute-start.1 = (bf16[4,160,128]{2,1,0:T(8,128)(2,1)}, bf16[4,160,128]{2,1,0:T(8,128)(2,1)S(1)}, u32[]{:S(2)}, u32[]{:S(2)}) collective-permute-start(bf16[4,160,128]{2,1,0:T(8,128)(2,1)} %get-tuple-element.22), channel_id=1, source_target_pairs={{0,4},{2,6},{4,8},{6,10},{8,12},{10,14},{12,16},{14,18},{16,20},{1... | collective-permute-start | bytes 491528 | tf_op jit(solution)/shard_map/ppermute | solution.py:578
  28.9 7.6 %collective-permute-start.2 = (bf16[4,160,128]{2,1,0:T(8,128)(2,1)}, bf16[4,160,128]{2,1,0:T(8,128)(2,1)S(1)}, u32[]{:S(2)}, u32[]{:S(2)}) collective-permute-start(bf16[4,160,128]{2,1,0:T(8,128)(2,1)} %get-tuple-element.22), channel_id=1, source_target_pairs={{0,6},{2,8},{4,10},{6,12},{8,14},{10,16},{12,18},{14,20},{16,22},{... | collective-permute-start | bytes 491528 | tf_op jit(solution)/shard_map/ppermute | solution.py:578
  36.6 3.0 %collective-permute-start.3 = (bf16[4,160,128]{2,1,0:T(8,128)(2,1)}, bf16[4,160,128]{2,1,0:T(8,128)(2,1)S(1)}, u32[]{:S(2)}, u32[]{:S(2)}) collective-permute-start(bf16[4,160,128]{2,1,0:T(8,128)(2,1)} %get-tuple-element.23), channel_id=1, source_target_pairs={{2,0},{4,2},{6,4},{8,6},{10,8},{12,10},{14,12},{16,14},{18,16},{20... | collective-permute-start | bytes 491528 | tf_op jit(solution)/shard_map/ppermute | solution.py:581
  39.6 2.2 %collective-permute-start.4 = (bf16[4,160,128]{2,1,0:T(8,128)(2,1)}, bf16[4,160,128]{2,1,0:T(8,128)(2,1)S(1)}, u32[]{:S(2)}, u32[]{:S(2)}) collective-permute-start(bf16[4,160,128]{2,1,0:T(8,128)(2,1)} %get-tuple-element.23), channel_id=1, source_target_pairs={{4,0},{6,2},{8,4},{10,6},{12,8},{14,10},{16,12},{18,14},{20,16},{2... | collective-permute-start | bytes 491528 | tf_op jit(solution)/shard_map/ppermute | solution.py:581
  41.8 0.0 copy-done.5
  41.8 0.1 dynamic_slice.3
  41.9 0.2 fusion
  42.1 0.0 collective-permute-done.got_l1
  42.1 1.9 %collective-permute-start.5 = (bf16[4,160,128]{2,1,0:T(8,128)(2,1)}, bf16[4,160,128]{2,1,0:T(8,128)(2,1)S(1)}, u32[]{:S(2)}, u32[]{:S(2)}) collective-permute-start(bf16[4,160,128]{2,1,0:T(8,128)(2,1)} %get-tuple-element.23), channel_id=1, source_target_pairs={{6,0},{8,2},{10,4},{12,6},{14,8},{16,10},{18,12},{20,14},{22,16},{... | collective-permute-start | bytes 491528 | tf_op jit(solution)/shard_map/ppermute | solution.py:581
  44.0 0.0 copy-done.8
  44.0 0.0 copy-done.9
  44.0 0.0 copy-start.6
  44.0 1.2 %copy-done.6 = bf16[3584,128]{1,0:T(8,128)(2,1)S(1)} copy-done((bf16[3584,128]{1,0:T(8,128)(2,1)S(1)}, bf16[3584,128]{1,0:T(8,128)(2,1)}, u32[]{:S(2)}) %copy-start.6) | copy-done | bytes 917528
  45.2 0.0 copy-start.7
  45.2 1.2 %copy-done.7 = bf16[3584,128]{1,0:T(8,128)(2,1)S(1)} copy-done((bf16[3584,128]{1,0:T(8,128)(2,1)S(1)}, bf16[3584,128]{1,0:T(8,128)(2,1)}, u32[]{:S(2)}) %copy-start.7) | copy-done | bytes 917528
  46.4 0.0 copy-start
  46.4 0.0 copy-start.3
  46.4 0.0 copy-start.4
  46.4 22.7 %attention.1 = (bf16[2048,128]{1,0:T(8,128)(2,1)}, f32[3584,128]{1,0:T(8,128)}, f32[3584,128]{1,0:T(8,128)}) custom-call(s32[2]{0:T(128)S(1)} %subtract_add_fusion.spot, bf16[2048,128]{1,0:T(8,128)(2,1)S(1)} %bitcast.13, bf16[2048,128]{1,0:T(8,128)(2,1)S(1)} %bitcast.14, bf16[3584,128]{1,0:T(8,128)(2,1)S(1)} %copy-done.6, bf16[3584,128]{1,0:T(8,128)(2,1)S(1)} %copy-done.7), custom_call_target="tpu_custom_call" | custom-call | flops 9395240960 | bytes 3670016 | tf_op jit(solution)/shard_map/attention/pallas_call | solution.py:532
  69.1 0.0 collective-permute-done.1.got_l2
  69.1 0.0 collective-permute-done.2.got_l3
  69.1 0.0 collective-permute-done.3.got_r1
  69.1 0.0 collective-permute-done.4.got_r2
  69.1 0.0 collective-permute-done.5.got_r3
  69.1 0.0 copy-done
  69.1 0.0 copy-done.3
  69.1 0.0 copy-done.4
  69.2 0.0 copy-start.1
  69.2 1.5 %copy-done.1 = f32[3584,128]{1,0:T(8,128)S(1)} copy-done((f32[3584,128]{1,0:T(8,128)S(1)}, f32[3584,128]{1,0:T(8,128)}, u32[]{:S(2)}) %copy-start.1) | copy-done | bytes 1835032
  70.7 0.0 copy-start.2
  70.7 1.5 %copy-done.2 = f32[3584,128]{1,0:T(8,128)S(1)} copy-done((f32[3584,128]{1,0:T(8,128)S(1)}, f32[3584,128]{1,0:T(8,128)}, u32[]{:S(2)}) %copy-start.2) | copy-done | bytes 1835032
  72.2 38.8 %reduce.1 = (bf16[2048,128]{1,0:T(8,128)(2,1)S(1)}, bf16[2048,128]{1,0:T(8,128)(2,1)S(1)}, bf16[2048,128]{1,0:T(8,128)(2,1)S(1)}, bf16[256,128]{1,0:T(8,128)(2,1)S(1)}, bf16[256,128]{1,0:T(8,128)(2,1)S(1)}) custom-call(s32[32]{0:T(128)S(1)} %copy-done.5, f32[4,512]{1,0:T(4,128)S(1)} %copy-done.4, bf16[4,2,4,256,128]{4,3,2,1,0:T(8,128)(2,1)S(1)} %copy-done, ...), custom_call_target="tpu_custom_call" | custom-call | tf_op jit(solution)/shard_map/reduce/pallas_call | solution.py:590
  111.0 0.8 copy.21
  111.8 0.8 copy.22
  112.5 0.8 copy.23
  113.3 0.6 copy.24
  114.0 0.6 copy.25
  (1 shorter events, 0.0 us)
Async XLA Ops:
  0.6 41.1 %copy-start.5 = (s32[32]{0:T(128)S(1)}, s32[32]{0:T(128)}, u32[]{:S(2)}) copy-start(s32[32]{0:T(128)} %doc.3) | copy-start | bytes 388
  0.6 43.3 %copy-start.8 = (bf16[512,4,128]{2,1,0:T(4,128)(2,1)S(1)}, bf16[512,4,128]{2,1,0:T(4,128)(2,1)}, u32[]{:S(2)}) copy-start(bf16[512,4,128]{2,1,0:T(4,128)(2,1)} %param.15) | copy-start | bytes 1572868
  0.7 43.3 %copy-start.9 = (bf16[512,4,128]{2,1,0:T(4,128)(2,1)S(1)}, bf16[512,4,128]{2,1,0:T(4,128)(2,1)}, u32[]{:S(2)}) copy-start(bf16[512,4,128]{2,1,0:T(4,128)(2,1)} %param.18) | copy-start | bytes 1572868
  22.7 19.4 %collective-permute-start = (bf16[4,160,128]{2,1,0:T(8,128)(2,1)}, bf16[4,160,128]{2,1,0:T(8,128)(2,1)S(1)}, u32[]{:S(2)}, u32[]{:S(2)}) collective-permute-start(bf16[4,160,128]{2,1,0:T(8,128)(2,1)} %get-tuple-element.22), channel_id=1, source_target_pairs={{0,2},{2,4},{4,6},{6,8},{8,10},{10,12},{12,14},{14,16},{16,18},{18... | collective-permute-start | bytes 491528 | tf_op jit(solution)/shard_map/ppermute | solution.py:578
  24.6 44.5 %collective-permute-start.1 = (bf16[4,160,128]{2,1,0:T(8,128)(2,1)}, bf16[4,160,128]{2,1,0:T(8,128)(2,1)S(1)}, u32[]{:S(2)}, u32[]{:S(2)}) collective-permute-start(bf16[4,160,128]{2,1,0:T(8,128)(2,1)} %get-tuple-element.22), channel_id=1, source_target_pairs={{0,4},{2,6},{4,8},{6,10},{8,12},{10,14},{12,16},{14,18},{16,20},{1... | collective-permute-start | bytes 491528 | tf_op jit(solution)/shard_map/ppermute | solution.py:578
  28.9 40.2 %collective-permute-start.2 = (bf16[4,160,128]{2,1,0:T(8,128)(2,1)}, bf16[4,160,128]{2,1,0:T(8,128)(2,1)S(1)}, u32[]{:S(2)}, u32[]{:S(2)}) collective-permute-start(bf16[4,160,128]{2,1,0:T(8,128)(2,1)} %get-tuple-element.22), channel_id=1, source_target_pairs={{0,6},{2,8},{4,10},{6,12},{8,14},{10,16},{12,18},{14,20},{16,22},{... | collective-permute-start | bytes 491528 | tf_op jit(solution)/shard_map/ppermute | solution.py:578
  36.6 32.5 %collective-permute-start.3 = (bf16[4,160,128]{2,1,0:T(8,128)(2,1)}, bf16[4,160,128]{2,1,0:T(8,128)(2,1)S(1)}, u32[]{:S(2)}, u32[]{:S(2)}) collective-permute-start(bf16[4,160,128]{2,1,0:T(8,128)(2,1)} %get-tuple-element.23), channel_id=1, source_target_pairs={{2,0},{4,2},{6,4},{8,6},{10,8},{12,10},{14,12},{16,14},{18,16},{20... | collective-permute-start | bytes 491528 | tf_op jit(solution)/shard_map/ppermute | solution.py:581
  39.6 29.5 %collective-permute-start.4 = (bf16[4,160,128]{2,1,0:T(8,128)(2,1)}, bf16[4,160,128]{2,1,0:T(8,128)(2,1)S(1)}, u32[]{:S(2)}, u32[]{:S(2)}) collective-permute-start(bf16[4,160,128]{2,1,0:T(8,128)(2,1)} %get-tuple-element.23), channel_id=1, source_target_pairs={{4,0},{6,2},{8,4},{10,6},{12,8},{14,10},{16,12},{18,14},{20,16},{2... | collective-permute-start | bytes 491528 | tf_op jit(solution)/shard_map/ppermute | solution.py:581
  42.1 27.1 %collective-permute-start.5 = (bf16[4,160,128]{2,1,0:T(8,128)(2,1)}, bf16[4,160,128]{2,1,0:T(8,128)(2,1)S(1)}, u32[]{:S(2)}, u32[]{:S(2)}) collective-permute-start(bf16[4,160,128]{2,1,0:T(8,128)(2,1)} %get-tuple-element.23), channel_id=1, source_target_pairs={{6,0},{8,2},{10,4},{12,6},{14,8},{16,10},{18,12},{20,14},{22,16},{... | collective-permute-start | bytes 491528 | tf_op jit(solution)/shard_map/ppermute | solution.py:581
  44.0 1.2 %copy-start.6 = (bf16[3584,128]{1,0:T(8,128)(2,1)S(1)}, bf16[3584,128]{1,0:T(8,128)(2,1)}, u32[]{:S(2)}) copy-start(bf16[3584,128]{1,0:T(8,128)(2,1)} %get-tuple-element.24.keys_in) | copy-start | bytes 2752516
  45.2 1.2 %copy-start.7 = (bf16[3584,128]{1,0:T(8,128)(2,1)S(1)}, bf16[3584,128]{1,0:T(8,128)(2,1)}, u32[]{:S(2)}) copy-start(bf16[3584,128]{1,0:T(8,128)(2,1)} %get-tuple-element.25.values) | copy-start | bytes 2752516
  46.4 22.8 %copy-start = (bf16[4,2,4,256,128]{4,3,2,1,0:T(8,128)(2,1)S(1)}, bf16[4,2,4,256,128]{4,3,2,1,0:T(8,128)(2,1)}, u32[]{:S(2)}) copy-start(bf16[4,2,4,256,128]{4,3,2,1,0:T(8,128)(2,1)} %get-tuple-element.20.parts) | copy-start | bytes 6291460
  46.4 22.8 %copy-start.3 = (f32[2,2,4,128,128]{4,3,2,1,0:T(8,128)S(1)}, f32[2,2,4,128,128]{4,3,2,1,0:T(8,128)}, u32[]{:S(2)}) copy-start(f32[2,2,4,128,128]{4,3,2,1,0:T(8,128)} %get-tuple-element.21.states) | copy-start | bytes 3145732
  46.4 22.8 %copy-start.4 = (f32[4,512]{1,0:T(4,128)S(1)}, f32[4,512]{1,0:T(4,128)}, u32[]{:S(2)}) copy-start(f32[4,512]{1,0:T(4,128)} %dec.1) | copy-start | bytes 24580
  69.2 1.5 %copy-start.1 = (f32[3584,128]{1,0:T(8,128)S(1)}, f32[3584,128]{1,0:T(8,128)}, u32[]{:S(2)}) copy-start(f32[3584,128]{1,0:T(8,128)} %get-tuple-element.26.dkey) | copy-start | bytes 5505028
  70.7 1.5 %copy-start.2 = (f32[3584,128]{1,0:T(8,128)S(1)}, f32[3584,128]{1,0:T(8,128)}, u32[]{:S(2)}) copy-start(f32[3584,128]{1,0:T(8,128)} %get-tuple-element.27.dvalue) | copy-start | bytes 5505028
